TPU v7x, 512 devices: a whole 4x4x16 slice. The times are simulated.
512 devices in a mesh: turn: 64 (over y, z_lo, core), head: 8 (over z_hi, x).
Axes of the slice: x: 4, y: 4, z: 16 (z_hi: 2, z_lo: 8; z = z_hi * 8 + z_lo), core: 2. Of those that a mesh axis runs over, the one named last changes fastest.
Arguments:
- query: bfloat16 [32768, 8192], P('turn', 'head'), may hold values from -6 to 6
- vision: bfloat16 [1024, 8192], P(None, 'turn'), may hold values from -6 to 6
- w_key: bfloat16 [8192, 1024], P('turn', 'head'), may hold values from -0.0625 to 0.0625
- w_value: bfloat16 [8192, 1024], P('turn', 'head'), may hold values from -0.0625 to 0.0625
- q_gain: float32 [128], replicated, may hold values from 0.8 to 2.2
- k_gain: float32 [128], replicated, may hold values from 0.8 to 2.2
- text_turn: int32 [32768], P('turn'), may hold values from 0 to 63, never falling along the last dimension, each value on 1 to 1024 neighbouring positions
- tile_turn: int32 [4], replicated, may hold values from 0 to 63, as said below
- tile_len: int32 [4], replicated, may hold values from 128 to 256, as said below
- grad_out: bfloat16 [32768, 8192], P('turn', 'head'), may hold values from -6 to 6
Outputs:
- attended: bfloat16 [32768, 8192], P('turn', 'head')
- grad_query: bfloat16 [32768, 8192], P('turn', 'head')
- grad_vision: bfloat16 [1024, 8192], P('head', 'turn')
- grad_w_key: float32 [8192, 1024], P('turn', 'head')
- grad_w_value: float32 [8192, 1024], P('turn', 'head')
Inputs may be any that keep to these rules, and one draw needn't show every extreme that they name: `text_turn`: never falling along the dialogue; every turn holds 1 to 1024 tokens. `tile_turn`: some tile is shown at turn 0. `tile_len`: some tile is full.
All inputs are finite; a program needn't handle non-finite values.
Results may differ from a plain program's by a relative error of at most 0.02.
Values may be sent and summed in bfloat16 or wider, within the bound.
A program may use at most 64 MiB of HBM per device.

v0:
```python
import math

import jax
import jax.numpy as jnp
from jax import lax
from jax.sharding import PartitionSpec as P

HD = 128
TILE_TOK = 256
TURNS = 64


epsilon = 1e-05


def norm_rows(values, gain):
    inverse = lax.rsqrt(jnp.mean(values * values, axis=-1, keepdims=True) + epsilon)
    return (values * inverse * gain, inverse)


def norm_back(values, inverse, gain, upstream):
    scaled = upstream * gain
    return inverse * scaled - values * inverse**3 * jnp.mean(
        values * scaled, axis=-1, keepdims=True
    )


def key_turns(tile_turn, tile_len, slot_count, tile_size):
    position = jnp.arange(slot_count, dtype=jnp.int32)
    which = position // tile_size
    inside = position - which * tile_size
    onehot = which[:, None] == jnp.arange(tile_turn.shape[0], dtype=jnp.int32)[None, :]
    shown = jnp.sum(jnp.where(onehot, tile_turn[None, :], 0), axis=1)
    length = jnp.sum(jnp.where(onehot, tile_len[None, :], 0), axis=1)
    return jnp.where(inside < length, shown, TURNS)


def body(query, vision, w_key, w_value, q_gain, k_gain, text_turn, tile_turn, tile_len, grad_out):
    text_rows = query.shape[0]
    head_count = query.shape[1] // HD
    kv_count = w_key.shape[1] // HD
    group = head_count // kv_count
    slot_count = vision.shape[0]
    width_kv = kv_count * HD
    scale = 1.0 / math.sqrt(HD)
    q_float = query.astype(jnp.float32).reshape(text_rows, head_count, HD)
    q_normed, q_inverse = norm_rows(q_float, q_gain)
    q_cast = q_normed.astype(jnp.bfloat16)
    weights_kv = jnp.concatenate([w_key, w_value], axis=1)
    kv_summed = lax.psum(jnp.dot(vision, weights_kv, preferred_element_type=jnp.float32), "turn")
    k_raw = kv_summed[:, :width_kv].reshape(slot_count, kv_count, HD)
    k_normed, k_inverse = norm_rows(k_raw, k_gain)
    kv_cast = jnp.concatenate(
        [k_normed.reshape(slot_count, width_kv), kv_summed[:, width_kv:]], axis=1
    ).astype(jnp.bfloat16)
    k_cast = kv_cast[:, :width_kv].reshape(slot_count, kv_count, HD)
    v_cast = kv_cast[:, width_kv:].reshape(slot_count, kv_count, HD)
    allowed = key_turns(tile_turn, tile_len, slot_count, TILE_TOK)[None, :] <= text_turn[:, None]
    upstream = grad_out.reshape(text_rows, head_count, HD)

    def one_head(carry, head):
        key_acc, value_acc = carry
        kv_index = head // group
        q_head = lax.dynamic_index_in_dim(q_cast, head, 1, keepdims=False)
        qf_head = lax.dynamic_index_in_dim(q_float, head, 1, keepdims=False)
        qi_head = lax.dynamic_index_in_dim(q_inverse, head, 1, keepdims=False)
        up_head = lax.dynamic_index_in_dim(upstream, head, 1, keepdims=False)
        k_head = lax.dynamic_index_in_dim(k_cast, kv_index, 1, keepdims=False)
        v_head = lax.dynamic_index_in_dim(v_cast, kv_index, 1, keepdims=False)
        scores = (
            lax.dot_general(
                q_head, k_head, (((1,), (1,)), ((), ())), preferred_element_type=jnp.float32
            )
            * scale
        )
        expo = jnp.where(allowed, jnp.exp(scores), 0.0)
        probs = (expo / jnp.sum(expo, axis=1, keepdims=True)).astype(jnp.bfloat16)
        attended_head = jnp.dot(probs, v_head, preferred_element_type=jnp.float32).astype(
            jnp.bfloat16
        )
        d_probs = lax.dot_general(
            up_head, v_head, (((1,), (1,)), ((), ())), preferred_element_type=jnp.float32
        )
        delta = jnp.sum(
            up_head.astype(jnp.float32) * attended_head.astype(jnp.float32), axis=1, keepdims=True
        )
        d_scores = (probs.astype(jnp.float32) * (d_probs - delta)).astype(jnp.bfloat16)
        d_query = jnp.dot(d_scores, k_head, preferred_element_type=jnp.float32) * scale
        grad_head = norm_back(qf_head, qi_head, q_gain, d_query).astype(jnp.bfloat16)
        d_key = (
            lax.dot_general(
                d_scores, q_head, (((0,), (0,)), ((), ())), preferred_element_type=jnp.float32
            )
            * scale
        )
        d_value = lax.dot_general(
            probs, up_head, (((0,), (0,)), ((), ())), preferred_element_type=jnp.float32
        )
        key_acc = key_acc.at[kv_index].add(d_key)
        value_acc = value_acc.at[kv_index].add(d_value)
        return ((key_acc, value_acc), (attended_head, grad_head))

    zeros = jnp.zeros((kv_count, slot_count, HD), jnp.float32)
    (key_acc, value_acc), (att_heads, grad_heads) = lax.scan(
        one_head, (zeros, zeros), jnp.arange(head_count, dtype=jnp.int32)
    )
    attended = att_heads.transpose(1, 0, 2).reshape(text_rows, head_count * HD)
    grad_query = grad_heads.transpose(1, 0, 2).reshape(text_rows, head_count * HD)
    d_terms = jnp.concatenate(
        [
            key_acc.transpose(1, 0, 2).reshape(slot_count, width_kv),
            value_acc.transpose(1, 0, 2).reshape(slot_count, width_kv),
        ],
        axis=1,
    )
    d_summed = lax.psum(d_terms, "turn")
    d_key_raw = norm_back(
        k_raw, k_inverse, k_gain, d_summed[:, :width_kv].reshape(slot_count, kv_count, HD)
    )
    d_cast = jnp.concatenate(
        [d_key_raw.reshape(slot_count, width_kv), d_summed[:, width_kv:]], axis=1
    ).astype(jnp.bfloat16)
    grad_both = lax.dot_general(
        vision, d_cast, (((0,), (0,)), ((), ())), preferred_element_type=jnp.float32
    )
    grad_w_key = grad_both[:, :width_kv]
    grad_w_value = grad_both[:, width_kv:]
    grad_vision = lax.psum_scatter(
        lax.dot_general(
            d_cast, weights_kv, (((1,), (1,)), ((), ())), preferred_element_type=jnp.float32
        ).astype(jnp.bfloat16),
        "head",
        scatter_dimension=0,
        tiled=True,
    )
    return (attended, grad_query, grad_vision, grad_w_key, grad_w_value)


def solution(mesh):
    return jax.shard_map(
        body,
        mesh=mesh,
        in_specs=(
            P("turn", "head"),
            P(None, "turn"),
            P("turn", "head"),
            P("turn", "head"),
            P(),
            P(),
            P("turn"),
            P(),
            P(),
            P("turn", "head"),
        ),
        out_specs=(
            P("turn", "head"),
            P("turn", "head"),
            P("head", "turn"),
            P("turn", "head"),
            P("turn", "head"),
        ),
        check_vma=False,
    )
```

profile of v0, /device:TPU:16, one launch (start us, length us, event | category | flops | bytes accessed | tf_op | source)
XLA Modules:
  0.0 1941.1 jit_solution(2585367353282851265)
XLA Ops:
  10.9 1.7 copy.37
  12.6 1.9 multiply_reduce_fusion.1
  14.5 1.3 copy.38
  16.6 3.0 multiply_convert_fusion.1
  19.7 790.0 %all-reduce.3.cloned.1.call-done = f32[1024,256]{0,1:T(8,128)} async-done(((f32[1024,256]{0,1:T(8,128)}), f32[1024,256]{0,1:T(8,128)}) %all-reduce.3.cloned.1.call-update) | async-done | bytes 1048592 | tf_op jit(solution)/shard_map/psum | solution.py:50
  815.1 143.2 %while.21 = (s32[]{:T(128)}, f32[1,1024,128]{2,1,0:T(8,128)S(1)}, f32[1,1024,128]{2,1,0:T(8,128)}, bf16[8,512,128]{1,2,0:T(8,128)(2,1)}, bf16[8,512,128]{1,2,0:T...) while((s32[]{:T(128)}, f32[1,1024,128]{2,1,0:T(8,128)S(1)}, ...), condition=%wide.region_10.11_spmd.clone, body=%wide.region_5.10_spmd.clone.sunk | while | flops 812318848 | bytes 21142580 | solution.py:104
  818.1 1.6 fusion.69
  820.1 1.4 multiply_reduce_fusion.5
  821.5 1.4 multiply_convert_fusion.4
  825.3 2.2 fusion.70
  827.5 2.1 fusion.71
  829.7 1.6 fusion.72
  831.3 1.7 fusion.73
  836.0 1.6 fusion.69
  838.0 1.4 multiply_reduce_fusion.5
  839.4 1.4 multiply_convert_fusion.4
  843.2 2.2 fusion.70
  845.4 2.1 fusion.71
  847.5 1.6 fusion.72
  849.2 1.7 fusion.73
  853.9 1.6 fusion.69
  855.8 1.4 multiply_reduce_fusion.5
  857.2 1.4 multiply_convert_fusion.4
  861.1 2.2 fusion.70
  863.3 2.1 fusion.71
  865.4 1.6 fusion.72
  867.1 1.7 fusion.73
  871.8 1.6 fusion.69
  873.7 1.4 multiply_reduce_fusion.5
  875.1 1.4 multiply_convert_fusion.4
  879.0 2.2 fusion.70
  881.2 2.1 fusion.71
  883.3 1.6 fusion.72
  885.0 1.7 fusion.73
  889.7 1.7 fusion.69
  891.6 1.4 multiply_reduce_fusion.5
  893.1 1.4 multiply_convert_fusion.4
  896.9 2.2 fusion.70
  899.1 2.1 fusion.71
  901.3 1.6 fusion.72
  902.9 1.7 fusion.73
  907.6 1.6 fusion.69
  909.6 1.4 multiply_reduce_fusion.5
  911.0 1.4 multiply_convert_fusion.4
  914.8 2.2 fusion.70
  917.0 2.1 fusion.71
  919.2 1.6 fusion.72
  920.8 1.7 fusion.73
  925.5 1.6 fusion.69
  927.5 1.4 multiply_reduce_fusion.5
  928.9 1.4 multiply_convert_fusion.4
  932.7 2.2 fusion.70
  934.9 2.1 fusion.71
  937.1 1.6 fusion.72
  938.7 1.7 fusion.73
  943.4 1.6 fusion.69
  945.4 1.4 multiply_reduce_fusion.5
  946.8 1.4 multiply_convert_fusion.4
  950.6 2.2 fusion.70
  952.8 2.1 fusion.71
  955.0 1.6 fusion.72
  956.6 1.7 fusion.73
  961.0 827.2 %all-reduce.5.cloned.1.call-done = f32[1024,256]{0,1:T(8,128)} async-done(((f32[1024,256]{0,1:T(8,128)}), f32[1024,256]{0,1:T(8,128)}) %all-reduce.5.cloned.1.call-update) | async-done | bytes 1048592 | tf_op jit(solution)/shard_map/psum | solution.py:116
  1797.2 137.4 %reduce-scatter.2.cloned.1.call-done = bf16[128,128]{1,0:T(8,128)(2,1)} async-done(((bf16[1024,128]{1,0:T(8,128)(2,1)}), bf16[128,128]{1,0:T(8,128)(2,1)}) %reduce-scatter.2.cloned.1.call-update) | async-done | bytes 32784 | tf_op jit(solution)/shard_map/reduce_scatter | solution.py:128
  (175 shorter events, 39.6 us)
Async XLA Ops:
  7.2 2.3 copy-start
  7.2 3.7 copy-start.4
  7.2 802.5 %all-reduce.3.cloned.1.call-start = ((), (), s32[]{:S(2)}) async-start(), calls=%async_computation.1 | async-start | bytes 2097152 | tf_op jit(solution)/shard_map/psum | solution.py:50
  8.9 0.6 copy-start.8
  10.9 3.7 copy-start.5
  10.9 1777.3 %all-reduce.5.cloned.1.call-start = ((), (), s32[]{:S(2)}) async-start(), calls=%async_computation.2 | async-start | bytes 2097152 | tf_op jit(solution)/shard_map/psum | solution.py:116
  12.6 3.3 copy-start.15
  12.6 3.4 copy-start.16
  12.6 4.1 copy-start.17
  15.9 796.1 %copy-start.13 = (f32[128]{0:T(128)S(1)}, f32[128]{0:T(128)}, u32[]{:S(2)}) copy-start(f32[128]{0:T(128)} %param.21) | copy-start | bytes 1540
  811.4 0.6 copy-start.10
  824.6 2.9 copy-start.1
  825.3 4.3 copy-start.18
  829.6 3.4 copy-start.2
  842.5 2.9 copy-start.1
  843.2 4.3 copy-start.18
  847.5 3.4 copy-start.2
  860.4 2.9 copy-start.1
  861.1 4.3 copy-start.18
  865.4 3.4 copy-start.2
  878.3 2.9 copy-start.1
  879.0 4.3 copy-start.18
  883.3 3.4 copy-start.2
  896.2 2.9 copy-start.1
  896.9 4.3 copy-start.18
  901.2 3.4 copy-start.2
  914.1 2.9 copy-start.1
  914.8 4.3 copy-start.18
  919.1 3.4 copy-start.2
  932.0 2.9 copy-start.1
  932.7 4.3 copy-start.18
  937.0 3.4 copy-start.2
  949.9 2.9 copy-start.1
  950.6 4.3 copy-start.18
  954.9 3.4 copy-start.2
  959.6 828.6 %copy-start.3 = (f32[1024,256]{0,1:T(8,128)S(1)}, f32[1024,256]{0,1:T(8,128)}, u32[]{:S(2)}) copy-start(f32[1024,256]{0,1:T(8,128)} %all-reduce.3.cloned.1.call-done) | copy-start | bytes 3145732
  959.6 828.6 %copy-start.14 = (f32[128]{0:T(128)S(1)}, f32[128]{0:T(128)}, u32[]{:S(2)}) copy-start(f32[128]{0:T(128)} %param.21) | copy-start | bytes 1540
  959.8 830.7 %copy-start.11 = (f32[1024]{0:T(1024)S(1)}, f32[1024]{0:T(1024)}, u32[]{:S(2)}) copy-start(f32[1024]{0:T(1024)} %copy-done.10) | copy-start | bytes 12292
  959.8 830.7 %copy-start.12 = (f32[1024]{0:T(1024)S(1)}, f32[1024]{0:T(1024)}, u32[]{:S(2)}) copy-start(f32[1024]{0:T(1024)} %get-tuple-element.364) | copy-start | bytes 12292
  960.9 830.8 %copy-start.9 = (bf16[128,256]{1,0:T(8,128)(2,1)S(1)}, bf16[128,256]{1,0:T(8,128)(2,1)}, u32[]{:S(2)}) copy-start(bf16[128,256]{1,0:T(8,128)(2,1)} %copy-done.8) | copy-start | bytes 196612
  960.9 831.9 %copy-start.6 = (bf16[8,512,128]{1,2,0:T(8,128)(2,1)S(1)}, bf16[8,512,128]{1,2,0:T(8,128)(2,1)}, u32[]{:S(2)}) copy-start(bf16[8,512,128]{1,2,0:T(8,128)(2,1)} %get-tuple-element.206) | copy-start | bytes 3145732
  960.9 973.6 %reduce-scatter.2.cloned.1.call-start = ((), (), s32[]{:S(2)}) async-start(), calls=%async_computation.3 | async-start | bytes 294912 | tf_op jit(solution)/shard_map/reduce_scatter | solution.py:128
  1791.7 2.4 copy-start.7
Sparse Core Ops, SparseCore 0:
  11.0 798.6 all-reduce.2
  961.0 827.1 all-reduce.4
  1793.2 141.2 reduce-scatter.1
where the time goes:
time: 1940 us
  waiting for transfers between devices  1750 us (90%)
  matrix products  85.6 us (4%)
  other arithmetic  33.7 us (2%)
  loops' own time  28.3 us (1%)
  local copies, waits for them, and re-layouts  24.7 us (1%)
    psum x1, waiting for transfers between devices, body(): d_summed = lax.psum(d_terms, 'turn')  827 us
    psum x1, waiting for transfers between devices, body(): lax.psum(jnp.dot(vision, weights_kv, preferred_element_type=jnp.float32),...  790 us
    reduce_scatter x1, waiting for transfers between devices, body(): lax.psum_scatter(lax.dot_general(d_cast, weights_kv, (((1,), (1,)), ((),...  137 us
  transfers between devices with their start and end apart: 3, of which 3 were waited for; matrix products, arithmetic and copies ran while one was open for 1% of the time, Pallas kernels for 0%

commit v1 on v0

v1 whole, which is shorter than its diff:
```python
import functools
import math

import jax
import jax.numpy as jnp
from jax import lax
from jax.experimental import pallas as pl
from jax.experimental.pallas import tpu as pltpu
from jax.sharding import PartitionSpec as P

HD = 128
TILE_TOK = 256
TURNS = 64
EPS = 1e-05

NY, NZ, NC = 4, 8, 2
NHI, NX = 2, 4
SHARD = 16
CHUNK = NZ * SHARD
SLOTS = NC * NY * CHUNK

BF = jnp.bfloat16
F32 = jnp.float32
MESH = pl.DeviceIdType.MESH
SCALE = 1.0 / math.sqrt(HD)
LOG2E = math.log2(math.e)
MASKED = -16384.0
VMEM_LIMIT = 56 * 1024 * 1024

Y_ORDER = (2, 1, 3) if NY == 4 else tuple(range(1, NY))


def place():
    turn = lax.axis_index("turn")
    core = lax.rem(turn, NC)
    z = lax.rem(turn // NC, NZ)
    y = turn // (NC * NZ)
    return y, z, core


def turn_of(y, z, core):
    return (y * NZ + z) * NC + core


def remote(src, dst, send, recv, **where):
    return pltpu.make_async_remote_copy(
        src_ref=src, dst_ref=dst, send_sem=send, recv_sem=recv, device_id=where, device_id_type=MESH
    )


def turn_peers(y, z, core):
    peers = [turn_of(y, z, 1 - core)]
    peers += [turn_of(lax.rem(y + off, NY), z, core) for off in range(1, NY)]
    peers += [turn_of(y, lax.rem(z + off, NZ), core) for off in range(1, NZ)]
    return peers


def scatter_scratch():
    return [
        pltpu.VMEM((2, NY, CHUNK, HD), BF),
        pltpu.VMEM((2, NY, CHUNK, HD), BF),
        pltpu.VMEM((2, NY, CHUNK, HD), BF),
        pltpu.VMEM((2, NZ, SHARD, HD), F32),
        pltpu.VMEM((2, NZ, SHARD, HD), BF),
        pltpu.VMEM((2, NZ, SHARD, HD), BF),
        pltpu.SemaphoreType.DMA((2, 2, NY)),
        pltpu.SemaphoreType.DMA((2, 2, NY)),
        pltpu.SemaphoreType.DMA((2, 2, NZ)),
    ]


def gather_scratch():
    return [
        pltpu.SemaphoreType.DMA((2, 2, NZ)),
        pltpu.SemaphoreType.DMA((2, 2, NY)),
        pltpu.SemaphoreType.DMA((2, 2, NY)),
    ]


class Scatter:
    def __init__(self, refs, source, own):
        (self.from_c, self.to_y, self.from_y, self.total, self.to_z, self.from_z, self.sc, self.sy, self.sz) = refs
        self.source = source
        self.own = own
        self.sends = []

    def start(self, kind, off):
        y, z, core = place()
        yy = lax.rem(y + off, NY)
        copy = remote(
            self.source(kind, yy), self.from_c.at[kind, yy], self.sc.at[0, kind, off], self.sc.at[1, kind, off],
            turn=turn_of(y, z, 1 - core),
        )
        copy.start()
        self.sends.append(copy)

    def over_core(self, kind):
        y, z, core = place()
        for off in Y_ORDER + (0,):
            yy = lax.rem(y + off, NY)
            remote(
                self.source(kind, yy), self.from_c.at[kind, yy], self.sc.at[0, kind, off], self.sc.at[1, kind, off],
                turn=turn_of(y, z, 1 - core),
            ).wait_recv()
            both = self.own(kind, yy).astype(F32) + self.from_c[kind, yy].astype(F32)
            if off == 0:
                self.total[kind] = both.reshape(NZ, SHARD, HD)
                continue
            self.to_y[kind, off] = both.astype(BF)
            copy = remote(
                self.to_y.at[kind, off], self.from_y.at[kind, off], self.sy.at[0, kind, off], self.sy.at[1, kind, off],
                turn=turn_of(yy, z, core),
            )
            copy.start()
            self.sends.append(copy)

    def over_y(self, kind):
        y, z, core = place()
        total = self.total[kind].reshape(CHUNK, HD)
        for off in (1, 3, 2) if NY == 4 else range(1, NY):
            remote(
                self.to_y.at[kind, off], self.from_y.at[kind, off], self.sy.at[0, kind, off], self.sy.at[1, kind, off],
                turn=turn_of(y, z, core),
            ).wait_recv()
            total = total + self.from_y[kind, off].astype(F32)
        total = total.reshape(NZ, SHARD, HD)
        self.total[kind] = total
        self.to_z[kind] = total.astype(BF)
        for off in range(1, NZ):
            zz = lax.rem(z + off, NZ)
            copy = remote(
                self.to_z.at[kind, zz], self.from_z.at[kind, off], self.sz.at[0, kind, off], self.sz.at[1, kind, off],
                turn=turn_of(y, zz, core),
            )
            copy.start()
            self.sends.append(copy)

    def over_z(self, kind):
        y, z, core = place()
        total = self.total[kind, z]
        for off in range(1, NZ):
            remote(
                self.to_z.at[kind, off], self.from_z.at[kind, off], self.sz.at[0, kind, off], self.sz.at[1, kind, off],
                turn=turn_of(y, z, core),
            ).wait_recv()
            total = total + self.from_z[kind, off].astype(F32)
        return total

    def finish(self):
        for copy in self.sends:
            copy.wait_send()


class Gather:
    def __init__(self, refs, full):
        self.sz, self.sy, self.sc = refs
        self.full = full
        self.sends = []

    def go(self, src, sem, **where):
        copy = remote(src, src, sem[0], sem[1], **where)
        copy.start()
        self.sends.append(copy)

    def arrived(self, dst, sem):
        y, z, core = place()
        remote(dst, dst, sem[0], sem[1], turn=turn_of(y, z, 1 - core)).wait_recv()

    def over_z(self, kind, shard):
        y, z, core = place()
        self.full[kind, core, y, z] = shard.astype(BF)
        for off in range(1, NZ):
            self.go(
                self.full.at[kind, core, y, z], (self.sz.at[0, kind, off], self.sz.at[1, kind, off]),
                turn=turn_of(y, lax.rem(z + off, NZ), core),
            )

    def over_y(self, kind):
        y, z, core = place()
        for off in range(1, NZ):
            self.arrived(
                self.full.at[kind, core, y, lax.rem(z + NZ - off, NZ)], (self.sz.at[0, kind, off], self.sz.at[1, kind, off])
            )
        for off in Y_ORDER:
            self.go(
                self.full.at[kind, core, y], (self.sy.at[0, kind, off], self.sy.at[1, kind, off]),
                turn=turn_of(lax.rem(y + off, NY), z, core),
            )
        self.go(
            self.full.at[kind, core, y], (self.sc.at[0, kind, 0], self.sc.at[1, kind, 0]), turn=turn_of(y, z, 1 - core)
        )

    def over_core(self, kind, off):
        y, z, core = place()
        chunk = self.full.at[kind, core, lax.rem(y + NY - off, NY)]
        self.arrived(chunk, (self.sy.at[0, kind, off], self.sy.at[1, kind, off]))
        self.go(chunk, (self.sc.at[0, kind, off], self.sc.at[1, kind, off]), turn=turn_of(y, z, 1 - core))

    def last(self, kind, off):
        y, z, core = place()
        chunk = self.full.at[kind, 1 - core, lax.rem(y + NY - off, NY)]
        self.arrived(chunk, (self.sc.at[0, kind, off], self.sc.at[1, kind, off]))

    def finish(self):
        for copy in self.sends:
            copy.wait_send()


def inverse_rms(values):
    return lax.rsqrt(jnp.mean(values * values, axis=-1, keepdims=True) + EPS)


def project_kernel(vision, w_key, w_value, k_gain, full, raw, to_c, own, *scratch):
    y, z, core = place()
    barrier = pltpu.get_barrier_semaphore()
    peers = turn_peers(y, z, core)
    for peer in peers:
        pl.semaphore_signal(barrier, inc=1, device_id={"turn": peer}, device_id_type=MESH)

    def partial(kind, cc, yy):
        weight = (w_key, w_value)[kind]
        return jnp.dot(vision[cc, yy], weight[...], preferred_element_type=F32)

    scatter = Scatter(scratch[:9], lambda kind, yy: to_c.at[kind, yy], lambda kind, yy: own[kind, yy])
    gather = Gather(scratch[9:], full)
    for kind in range(2):
        for off in range(NY):
            yy = lax.rem(y + off, NY)
            to_c[kind, yy] = partial(kind, 1 - core, yy).astype(BF)
    pl.semaphore_wait(barrier, len(peers))
    for kind in range(2):
        for off in Y_ORDER + (0,):
            scatter.start(kind, off)
    for kind in range(2):
        for off in range(NY):
            yy = lax.rem(y + off, NY)
            own[kind, yy] = partial(kind, core, yy)
    for kind in range(2):
        scatter.over_core(kind)
    for kind in range(2):
        scatter.over_y(kind)
    for kind in range(2):
        total = scatter.over_z(kind)
        if kind == 0:
            raw[...] = total
            total = total * inverse_rms(total) * k_gain[...]
        gather.over_z(kind, total)
    for kind in range(2):
        gather.over_y(kind)
    for off in (1, 3, 2) if NY == 4 else range(1, NY):
        for kind in range(2):
            gather.over_core(kind, off)
    for off in range(NY):
        for kind in range(2):
            gather.last(kind, off)
    scatter.finish()
    gather.finish()


def project(vision, w_key, w_value, k_gain):
    vmem = pl.BlockSpec(memory_space=pltpu.VMEM)
    return pl.pallas_call(
        project_kernel,
        out_shape=(
            jax.ShapeDtypeStruct((2, NC, NY, NZ, SHARD, HD), BF),
            jax.ShapeDtypeStruct((SHARD, HD), F32),
        ),
        in_specs=[vmem] * 4,
        out_specs=(vmem, vmem),
        scratch_shapes=[
            pltpu.VMEM((2, NY, CHUNK, HD), BF),
            pltpu.VMEM((2, NY, CHUNK, HD), F32),
        ]
        + scatter_scratch()
        + gather_scratch(),
        compiler_params=pltpu.CompilerParams(collective_id=0, has_side_effects=True, vmem_limit_bytes=VMEM_LIMIT),
        name="project",
    )(vision.reshape(NC, NY, CHUNK, vision.shape[1]), w_key, w_value, k_gain)


def attend_kernel(tile_turn, tile_len, query, grad_out, kv, text_turn, q_gain, attended, grad_query, d_kv, qa, ka, va, da, acc):
    step = pl.program_id(0)
    rows = query.shape[0]

    @pl.when(step == 0)
    def _():
        ka[:, :HD] = kv[0]
        va[:, :HD] = kv[1]
        va[:, HD:] = jnp.ones((SLOTS, HD), BF)
        for tile in range(SLOTS // TILE_TOK):
            inside = lax.broadcasted_iota(jnp.int32, (TILE_TOK, HD), 0)
            turn = lax.broadcasted_iota(jnp.int32, (TILE_TOK, HD), 1)
            shown = jnp.where(inside < tile_len[tile], tile_turn[tile], TURNS)
            hidden = jnp.logical_and(shown > turn, turn < TURNS)
            ka[pl.ds(tile * TILE_TOK, TILE_TOK), HD:] = jnp.where(hidden, MASKED, 0.0).astype(BF)
        turn = lax.broadcasted_iota(jnp.int32, (rows, HD), 1)
        qa[:, HD:] = jnp.where(text_turn[...] == turn, 1.0, 0.0).astype(BF)
        acc[...] = jnp.zeros_like(acc)

    gain = q_gain[...]
    q_float = query[...].astype(F32)
    inverse = inverse_rms(q_float)
    qa[:, :HD] = (q_float * inverse * gain * (SCALE * LOG2E)).astype(BF)
    scores = lax.dot_general(qa[...], ka[...], (((1,), (1,)), ((), ())), preferred_element_type=F32)
    expo = jnp.exp2(scores).astype(BF)
    summed = jnp.dot(expo, va[...], preferred_element_type=F32)
    over = 1.0 / summed[:, HD:]
    att = (summed[:, :HD] * over).astype(BF)
    attended[...] = att
    up = grad_out[...].astype(F32)
    delta = -jnp.sum(up * att.astype(F32), axis=1, keepdims=True) * over
    high = delta.astype(BF)
    low = (delta - high.astype(F32)).astype(BF)
    lane = lax.broadcasted_iota(jnp.int32, (rows, HD), 1)
    da[:, :HD] = (up * over).astype(BF)
    da[:, HD:] = jnp.where(lane == 0, high, jnp.where(lane == 1, low, jnp.zeros_like(low)))
    d_probs = lax.dot_general(da[...], va[...], (((1,), (1,)), ((), ())), preferred_element_type=F32)
    d_scores = expo * d_probs.astype(BF)
    d_query = jnp.dot(d_scores, ka[:, :HD], preferred_element_type=F32)
    scaled = d_query * (gain * SCALE)
    grad_query[...] = (
        inverse * scaled - q_float * (inverse * inverse * inverse) * jnp.mean(q_float * scaled, axis=1, keepdims=True)
    ).astype(BF)
    acc[0] += lax.dot_general(d_scores, qa[:, :HD], (((0,), (0,)), ((), ())), preferred_element_type=F32)
    acc[1] += lax.dot_general(expo, da[:, :HD], (((0,), (0,)), ((), ())), preferred_element_type=F32)

    @pl.when(step == pl.num_programs(0) - 1)
    def _():
        d_kv[0] = (acc[0] * (1.0 / LOG2E)).astype(BF)
        d_kv[1] = acc[1].astype(BF)


def attend(query, grad_out, kv, text_turn, tile_turn, tile_len, q_gain):
    rows, width = query.shape
    heads = width // HD
    smem = pl.BlockSpec(memory_space=pltpu.SMEM)
    block = pl.BlockSpec((rows, HD), lambda h: (0, h))

    def whole(*shape):
        return pl.BlockSpec(shape, lambda h: (0,) * len(shape))

    return pl.pallas_call(
        attend_kernel,
        grid=(heads,),
        out_shape=(
            jax.ShapeDtypeStruct(query.shape, BF),
            jax.ShapeDtypeStruct(query.shape, BF),
            jax.ShapeDtypeStruct((2, SLOTS, HD), BF),
        ),
        in_specs=[smem, smem, block, block, whole(2, SLOTS, HD), whole(rows, 1), whole(1, HD)],
        out_specs=(block, block, whole(2, SLOTS, HD)),
        scratch_shapes=[
            pltpu.VMEM((rows, 2 * HD), BF),
            pltpu.VMEM((SLOTS, 2 * HD), BF),
            pltpu.VMEM((SLOTS, 2 * HD), BF),
            pltpu.VMEM((rows, 2 * HD), BF),
            pltpu.VMEM((2, SLOTS, HD), F32),
        ],
        compiler_params=pltpu.CompilerParams(vmem_limit_bytes=VMEM_LIMIT),
        name="attend",
    )(tile_turn, tile_len, query, grad_out, kv, text_turn, q_gain)


def finish_kernel(
    d_kv, vision, w_key, w_value, raw, k_gain, grad_vision, grad_w_key, grad_w_value, full, to_x, from_x, to_hi, from_hi, sx, rx, sh, *scratch
):
    y, z, core = place()
    head = lax.axis_index("head")
    hi, x = head // NX, lax.rem(head, NX)
    barrier = pltpu.get_barrier_semaphore()
    peers = turn_peers(y, z, core)
    heads = [hi * NX + lax.rem(x + off, NX) for off in range(1, NX)] + [(1 - hi) * NX + x]
    for peer in peers:
        pl.semaphore_signal(barrier, inc=1, device_id={"turn": peer}, device_id_type=MESH)
    for peer in heads:
        pl.semaphore_signal(barrier, inc=1, device_id={"head": peer}, device_id_type=MESH)
    pl.semaphore_wait(barrier, len(peers) + len(heads))

    scatter = Scatter(
        scratch[:9], lambda kind, yy: d_kv.at[kind, 1 - core, yy], lambda kind, yy: d_kv[kind, core, yy]
    )
    gather = Gather(scratch[9:], full)
    for kind in range(2):
        for off in Y_ORDER + (0,):
            scatter.start(kind, off)
    for kind in range(2):
        scatter.over_core(kind)
    for kind in range(2):
        scatter.over_y(kind)
    for kind in range(2):
        total = scatter.over_z(kind)
        if kind == 0:
            raw_values = raw[...]
            inverse = inverse_rms(raw_values)
            scaled = total * k_gain[...]
            total = inverse * scaled - raw_values * (inverse * inverse * inverse) * jnp.mean(
                raw_values * scaled, axis=1, keepdims=True
            )
        gather.over_z(kind, total)
    for kind in range(2):
        gather.over_y(kind)

    def to_head(which, cc, off, yy):
        slot = lax.rem(yy - x + NX + NX - 1, NX)
        return remote(
            to_x.at[which, off], from_x.at[cc, slot], sx.at[which, off], rx.at[cc, slot], head=hi * NX + yy
        )

    def vision_term(which, off):
        cc = core if which == 0 else 1 - core
        yy = lax.rem(y + NY - off, NY)
        term = lax.dot_general(
            full[0, cc, yy].reshape(CHUNK, HD), w_key[...], (((1,), (1,)), ((), ())), preferred_element_type=F32
        ) + lax.dot_general(
            full[1, cc, yy].reshape(CHUNK, HD), w_value[...], (((1,), (1,)), ((), ())), preferred_element_type=F32
        )
        to_x[which, off] = term.astype(BF)

        @pl.when(yy != x)
        def _():
            to_head(which, cc, off, yy).start()

    vision_term(0, 0)
    order = (1, 3, 2) if NY == 4 else tuple(range(1, NY))
    for off in order:
        for kind in range(2):
            gather.over_core(kind, off)
        vision_term(0, off)
    for off in (0,) + order:
        for kind in range(2):
            gather.last(kind, off)
        vision_term(1, off)

    def summed(cc):
        total = to_x[lax.rem(cc + core, NC), lax.rem(y - x + NY, NY)].astype(F32)
        for slot in range(NX - 1):
            remote(from_x.at[cc, slot], from_x.at[cc, slot], sx.at[0, slot], rx.at[cc, slot], head=heads[0]).wait_recv()
            total = total + from_x[cc, slot].astype(F32)
        return total

    to_hi[...] = summed(1 - hi).astype(BF)
    over_hi = remote(to_hi, from_hi, sh.at[0], sh.at[1], head=(1 - hi) * NX + x)
    over_hi.start()
    kept = summed(hi)
    for kind, out in ((0, grad_w_key), (1, grad_w_value)):
        out[...] = lax.dot_general(
            vision[...], full[kind].reshape(SLOTS, HD), (((0,), (0,)), ((), ())), preferred_element_type=F32
        )
    over_hi.wait_recv()
    grad_vision[...] = (kept + from_hi[...].astype(F32)).astype(BF)
    over_hi.wait_send()
    for which in range(2):
        cc = core if which == 0 else 1 - core
        for off in range(NY):
            yy = lax.rem(y + NY - off, NY)

            @pl.when(yy != x)
            def _(which=which, cc=cc, off=off, yy=yy):
                to_head(which, cc, off, yy).wait_send()

    scatter.finish()
    gather.finish()


def finish(d_kv, vision, w_key, w_value, raw, k_gain):
    vmem = pl.BlockSpec(memory_space=pltpu.VMEM)
    width = vision.shape[1]
    return pl.pallas_call(
        finish_kernel,
        out_shape=(
            jax.ShapeDtypeStruct((CHUNK, width), BF),
            jax.ShapeDtypeStruct((width, HD), F32),
            jax.ShapeDtypeStruct((width, HD), F32),
        ),
        in_specs=[vmem] * 6,
        out_specs=(vmem,) * 3,
        scratch_shapes=[
            pltpu.VMEM((2, NC, NY, NZ, SHARD, HD), BF),
            pltpu.VMEM((2, NY, CHUNK, width), BF),
            pltpu.VMEM((2, NX, CHUNK, width), BF),
            pltpu.VMEM((CHUNK, width), BF),
            pltpu.VMEM((CHUNK, width), BF),
            pltpu.SemaphoreType.DMA((2, NY)),
            pltpu.SemaphoreType.DMA((2, NX)),
            pltpu.SemaphoreType.DMA((2,)),
        ]
        + scatter_scratch()
        + gather_scratch(),
        compiler_params=pltpu.CompilerParams(collective_id=1, has_side_effects=True, vmem_limit_bytes=VMEM_LIMIT),
        name="finish",
    )(d_kv.reshape(2, NC, NY, CHUNK, HD), vision, w_key, w_value, raw, k_gain)


def body(query, vision, w_key, w_value, q_gain, k_gain, text_turn, tile_turn, tile_len, grad_out):
    k_gain = k_gain.reshape(1, HD)
    full, raw = project(vision, w_key, w_value, k_gain)
    attended, grad_query, d_kv = attend(
        query, grad_out, full.reshape(2, SLOTS, HD), text_turn.reshape(-1, 1), tile_turn, tile_len, q_gain.reshape(1, HD)
    )
    grad_vision, grad_w_key, grad_w_value = finish(d_kv, vision, w_key, w_value, raw, k_gain)
    return (attended, grad_query, grad_vision, grad_w_key, grad_w_value)


def solution(mesh):
    return jax.shard_map(
        body,
        mesh=mesh,
        in_specs=(
            P("turn", "head"),
            P(None, "turn"),
            P("turn", "head"),
            P("turn", "head"),
            P(),
            P(),
            P("turn"),
            P(),
            P(),
            P("turn", "head"),
        ),
        out_specs=(
            P("turn", "head"),
            P("turn", "head"),
            P("head", "turn"),
            P("turn", "head"),
            P("turn", "head"),
        ),
        check_vma=False,
    )
```

time: 1940 us -> 112 us (0.06)
  the two profiles are of different devices: /device:TPU:16 before, /device:TPU:3 now
where the time goes in v1:
time: 112 us
  Pallas kernels  107 us (96%)
  local copies, waits for them, and re-layouts  4.42 us (4%)
    pallas_call x1, Pallas kernels, finish(): pl.pallas_call(finish_kernel, out_shape=(jax.ShapeDtypeStruct((CHUNK, wid...  44.2 us
    pallas_call x1, Pallas kernels, project(): pl.pallas_call(project_kernel, out_shape=(jax.ShapeDtypeStruct((2, NC, NY...  39.2 us
    pallas_call x1, Pallas kernels, attend(): pl.pallas_call(attend_kernel, grid=(heads,), out_shape=(jax.ShapeDtypeStr...  23.2 us
    unnamed x9, local copies, waits for them, and re-layouts  3.58 us

profile of v1, /device:TPU:3, one launch (start us, length us, event | category | flops | bytes accessed | tf_op | source)
XLA Modules:
  0.0 111.7 jit_solution(2679557186639329990)
XLA Ops:
  0.6 0.0 copy-start.2
  0.6 0.7 copy-done.2
  1.3 0.8 copy.15.text_turn
  2.2 39.2 %project.1 = (bf16[2,2,4,8,16,128]{5,4,3,2,1,0:T(8,128)(2,1)}, f32[16,128]{1,0:T(8,128)}) custom-call(bf16[2,4,128,128]{3,2,1,0:T(8,128)(2,1)} %bitcast.6, bf16[128,128]{1,0:T(8,128)(2,1)} %w_key.3, bf16[128,128]{1,0:T(8,128)(2,1)} %w_value.3, f32[1,128]{1,0:T(1,128)} %bitcast.10), custom_call_target="tpu_custom_call" | custom-call | tf_op jit(solution)/shard_map/project/pallas_call | solution.py:262
  41.4 23.2 %attend.1 = (bf16[512,1024]{1,0:T(8,128)(2,1)}, bf16[512,1024]{1,0:T(8,128)(2,1)}, bf16[2,1024,128]{2,1,0:T(8,128)(2,1)}) custom-call(s32[4]{0:T(128)} %tile_turn.1, s32[4]{0:T(128)} %tile_len.1, bf16[512,1024]{1,0:T(8,128)(2,1)} %query.1, bf16[512,1024]{1,0:T(8,128)(2,1)} %grad_out.1, bf16[2,1024,128]{2,1,0:T(8,128)(2,1)} %bitcast.8, ...), custom_call_target="tpu_custom_call" | custom-call | tf_op jit(solution)/shard_map/attend/pallas_call | solution.py:342
  64.6 44.2 %finish.1 = (bf16[128,128]{1,0:T(8,128)(2,1)}, f32[128,128]{1,0:T(8,128)}, f32[128,128]{1,0:T(8,128)}) custom-call(bf16[2,2,4,128,128]{4,3,2,1,0:T(8,128)(2,1)} %bitcast.7, bf16[1024,128]{1,0:T(8,128)(2,1)} %vision.1, bf16[128,128]{1,0:T(8,128)(2,1)} %w_key.3, bf16[128,128]{1,0:T(8,128)(2,1)} %w_value.3, f32[16,128]{1,0:T(8,128)} %get-tuple-element.17.raw, ...), custom_call_target="tpu_custom_call" | custom-call | tf_op jit(solution)/shard_map/finish/pallas_call | solution.py:468
  108.8 0.0 copy-start.1
  108.8 1.4 %copy.19 = bf16[128,128]{1,0:T(8,128)(2,1)} copy(bf16[128,128]{1,0:T(8,128)(2,1)} %get-tuple-element.28) | data formatting | bytes 65536
  110.2 0.0 copy-done.1
  110.2 0.0 copy-start
  110.2 0.6 copy.20
  110.8 0.2 copy-done
  111.1 0.6 copy.21
Async XLA Ops:
  0.6 0.7 copy-start.2
  108.8 1.4 %copy-start.1 = (f32[128,128]{1,0:T(8,128)S(1)}, f32[128,128]{1,0:T(8,128)}, u32[]{:S(2)}) copy-start(f32[128,128]{1,0:T(8,128)} %get-tuple-element.29) | copy-start | bytes 196612
  110.2 0.9 copy-start

commit v2 on v0

v2 whole, which is shorter than its diff:
```python
import math

import jax
import jax.numpy as jnp
from jax import lax
from jax.experimental import pallas as pl
from jax.experimental.pallas import tpu as pltpu
from jax.sharding import PartitionSpec as P

HD = 128
TILE_TOK = 256
TURNS = 64
EPS = 1e-05

NY, NZ, NC = 4, 8, 2
NHI, NX = 2, 4
CHUNK = 128
OWN_LO, OWNERS = 3, 2
SHARD = CHUNK // OWNERS
SLOTS = NC * NY * CHUNK

BF = jnp.bfloat16
F32 = jnp.float32
MESH = pl.DeviceIdType.MESH
SCALE = 1.0 / math.sqrt(HD)
LOG2E = math.log2(math.e)
MASKED = -16384.0
VMEM_LIMIT = 56 * 1024 * 1024

Y_ORDER = (2, 1, 3)
Y_ARRIVAL = (1, 3, 2)


def place():
    turn = lax.axis_index("turn")
    core = lax.rem(turn, NC)
    z = lax.rem(turn // NC, NZ)
    y = turn // (NC * NZ)
    return y, z, core


def turn_of(y, z, core):
    return (y * NZ + z) * NC + core


def is_owner(z):
    return jnp.logical_and(z >= OWN_LO, z < OWN_LO + OWNERS)


def remote(src, dst, send, recv, **where):
    return pltpu.make_async_remote_copy(
        src_ref=src, dst_ref=dst, send_sem=send, recv_sem=recv, device_id=where, device_id_type=MESH
    )


def scatter_scratch():
    return [
        pltpu.VMEM((2, NY, CHUNK, HD), BF),
        pltpu.VMEM((2, NY, CHUNK, HD), BF),
        pltpu.VMEM((2, NY, CHUNK, HD), BF),
        pltpu.VMEM((2, OWNERS, SHARD, HD), F32),
        pltpu.VMEM((2, OWNERS, SHARD, HD), BF),
        pltpu.VMEM((2, NZ, SHARD, HD), BF),
        pltpu.SemaphoreType.DMA((2, 2, NY)),
        pltpu.SemaphoreType.DMA((2, 2, NY)),
        pltpu.SemaphoreType.DMA((2, 2, NZ)),
    ]


def gather_scratch():
    return [
        pltpu.VMEM((2, NC, NY, OWNERS, SHARD, HD), BF),
        pltpu.SemaphoreType.DMA((2, 2, NZ)),
        pltpu.SemaphoreType.DMA((2, 2, NY)),
        pltpu.SemaphoreType.DMA((2, 2, NY)),
    ]


class Scatter:
    def __init__(self, refs, source, own):
        (self.from_c, self.to_y, self.from_y, self.total, self.to_z, self.from_z, self.sc, self.sy, self.sz) = refs
        self.source = source
        self.own = own

    def core_copy(self, kind, off):
        y, z, core = place()
        yy = lax.rem(y + off, NY)
        return remote(
            self.source(kind, yy), self.from_c.at[kind, yy], self.sc.at[0, kind, off], self.sc.at[1, kind, off],
            turn=turn_of(y, z, 1 - core),
        )

    def y_copy(self, kind, off):
        y, z, core = place()
        return remote(
            self.to_y.at[kind, off], self.from_y.at[kind, off], self.sy.at[0, kind, off], self.sy.at[1, kind, off],
            turn=turn_of(lax.rem(y + off, NY), z, core),
        )

    def z_copy(self, kind, step):
        y, z, core = place()
        far = z // (NZ // 2)
        owner = (OWNERS - 1 - step) * (1 - far) + step * far
        copy = remote(
            self.to_z.at[kind, owner], self.from_z.at[kind, z], self.sz.at[0, kind, owner], self.sz.at[1, kind, z],
            turn=turn_of(y, owner + OWN_LO, core),
        )
        return owner + OWN_LO != z, copy

    def start(self, kind):
        for off in Y_ORDER + (0,):
            self.core_copy(kind, off).start()

    def over_core(self, kind):
        y, z, core = place()
        for off in Y_ORDER + (0,):
            yy = lax.rem(y + off, NY)
            self.core_copy(kind, off).wait_recv()
            both = self.own(kind, yy).astype(F32) + self.from_c[kind, yy].astype(F32)
            if off == 0:
                self.total[kind] = both.reshape(OWNERS, SHARD, HD)
            else:
                self.to_y[kind, off] = both.astype(BF)
                self.y_copy(kind, off).start()

    def over_y(self, kind):
        total = self.total[kind].reshape(CHUNK, HD)
        for off in Y_ARRIVAL:
            self.y_copy(kind, off).wait_recv()
            total = total + self.from_y[kind, off].astype(F32)
        total = total.reshape(OWNERS, SHARD, HD)
        self.total[kind] = total
        self.to_z[kind] = total.astype(BF)
        for step in range(OWNERS):
            other, copy = self.z_copy(kind, step)

            @pl.when(other)
            def _(copy=copy):
                copy.start()

    def over_z(self, kind, then):
        y, z, core = place()

        @pl.when(is_owner(z))
        def _():
            total = self.total[kind, z - OWN_LO]
            for off in (1, 7, 2, 6, 3, 5, 4):
                zz = lax.rem(z + off, NZ)
                remote(
                    self.to_z.at[kind, 0], self.from_z.at[kind, zz], self.sz.at[0, kind, 0], self.sz.at[1, kind, zz],
                    turn=turn_of(y, zz, core),
                ).wait_recv()
                total = total + self.from_z[kind, zz].astype(F32)
            then(total)

    def finish(self):
        for kind in range(2):
            for off in range(NY):
                self.core_copy(kind, off).wait_send()
            for off in range(1, NY):
                self.y_copy(kind, off).wait_send()
            for step in range(OWNERS):
                other, copy = self.z_copy(kind, step)

                @pl.when(other)
                def _(copy=copy):
                    copy.wait_send()


class Gather:
    def __init__(self, refs):
        self.full, self.sz, self.sy, self.sc = refs

    def z_copy(self, kind, off):
        y, z, core = place()
        src = self.full.at[kind, core, y, z - OWN_LO]
        return remote(
            src, src, self.sz.at[0, kind, off], self.sz.at[1, kind, z - OWN_LO], turn=turn_of(y, lax.rem(z + off, NZ), core)
        )

    def y_copy(self, kind, off):
        y, z, core = place()
        src = self.full.at[kind, core, y]
        return remote(
            src, src, self.sy.at[0, kind, off], self.sy.at[1, kind, off], turn=turn_of(lax.rem(y + off, NY), z, core)
        )

    def core_copy(self, kind, off):
        y, z, core = place()
        src = self.full.at[kind, core, lax.rem(y + NY - off, NY)]
        return remote(src, src, self.sc.at[0, kind, off], self.sc.at[1, kind, off], turn=turn_of(y, z, 1 - core))

    def arrived(self, dst, sem):
        y, z, core = place()
        remote(dst, dst, sem[0], sem[1], turn=turn_of(y, z, 1 - core)).wait_recv()

    def over_z(self, kind, shard):
        y, z, core = place()
        self.full[kind, core, y, z - OWN_LO] = shard.astype(BF)
        for off in (4, 3, 5, 2, 6, 1, 7):
            self.z_copy(kind, off).start()

    def over_y(self, kind):
        y, z, core = place()
        for owner in range(OWNERS):

            @pl.when(z != owner + OWN_LO)
            def _(owner=owner):
                self.arrived(self.full.at[kind, core, y, owner], (self.sz.at[0, kind, 0], self.sz.at[1, kind, owner]))

        for off in Y_ORDER:
            self.y_copy(kind, off).start()
        self.core_copy(kind, 0).start()

    def over_core(self, kind, off):
        y, z, core = place()
        self.arrived(
            self.full.at[kind, core, lax.rem(y + NY - off, NY)], (self.sy.at[0, kind, off], self.sy.at[1, kind, off])
        )
        self.core_copy(kind, off).start()

    def last(self, kind, off):
        y, z, core = place()
        self.arrived(
            self.full.at[kind, 1 - core, lax.rem(y + NY - off, NY)], (self.sc.at[0, kind, off], self.sc.at[1, kind, off])
        )

    def finish(self):
        y, z, core = place()
        for kind in range(2):
            for off in range(1, NY):
                self.y_copy(kind, off).wait_send()
            for off in range(NY):
                self.core_copy(kind, off).wait_send()

            @pl.when(is_owner(z))
            def _(kind=kind):
                for off in range(1, NZ):
                    self.z_copy(kind, off).wait_send()


def inverse_rms(values):
    return lax.rsqrt(jnp.mean(values * values, axis=-1, keepdims=True) + EPS)


def rows_dot(a, b):
    return lax.dot_general(a, b, (((1,), (1,)), ((), ())), preferred_element_type=F32)


def columns_dot(a, b):
    return lax.dot_general(a, b, (((0,), (0,)), ((), ())), preferred_element_type=F32)


def cross_kernel(
    tile_turn, tile_len, query, grad_out, vision, w_key, w_value, text_turn, q_gain, k_gain,
    attended, grad_query, grad_vision, grad_w_key, grad_w_value,
    q_buf, up_buf, att_buf, gq_buf, s_in, s_out, qa, da, ka, va, inv, expo, slot_grad,
    to_c, own, raw, d_kv, to_x, from_x, to_hi, from_hi, sx, rx, sh, *scratch
):
    y, z, core = place()
    head = lax.axis_index("head")
    hi, x = head // NX, lax.rem(head, NX)
    heads, rows = q_buf.shape[0], q_buf.shape[1]

    barrier = pltpu.get_barrier_semaphore()

    def greet(**peer):
        pl.semaphore_signal(barrier, inc=1, device_id=peer, device_id_type=MESH)

    x_peers = [hi * NX + lax.rem(x + off, NX) for off in range(1, NX)]
    greet(head=(1 - hi) * NX + x)

    @pl.when(is_owner(z))
    def _():
        for off in range(1, NZ):
            greet(turn=turn_of(y, lax.rem(z + off, NZ), core))

    @pl.when(jnp.logical_not(is_owner(z)))
    def _():
        for owner in range(OWNERS):
            greet(turn=turn_of(y, owner + OWN_LO, core))

    for off in range(1, NY):
        greet(turn=turn_of(lax.rem(y + off, NY), z, core))
    for peer in x_peers:
        greet(head=peer)
    greet(turn=turn_of(y, z, 1 - core))

    def load(h, which):
        src, dst = ((query, q_buf), (grad_out, up_buf))[which]
        return pltpu.make_async_copy(src.at[:, pl.ds(h * HD, HD)], dst.at[h], s_in.at[which, h])

    def save(h, which):
        src, dst = ((att_buf, attended), (gq_buf, grad_query))[which]
        start = h * HD if isinstance(h, int) else pl.multiple_of(h * HD, HD)
        return pltpu.make_async_copy(src.at[h], dst.at[:, pl.ds(start, HD)], s_out.at[which, h])

    for which in range(2):
        for h in range(heads):
            load(h, which).start()

    def partial(kind, cc, yy):
        weight = (w_key, w_value)[kind]
        return jnp.dot(vision[cc, yy], weight[...], preferred_element_type=F32)

    for kind in range(2):
        for yy in range(NY):
            to_c[kind, yy] = partial(kind, 1 - core, yy).astype(BF)
            own[kind, yy] = partial(kind, core, yy)

    for tile in range(SLOTS // TILE_TOK):
        inside = lax.broadcasted_iota(jnp.int32, (TILE_TOK, HD), 0)
        turn = lax.broadcasted_iota(jnp.int32, (TILE_TOK, HD), 1)
        shown = jnp.where(inside < tile_len[tile], tile_turn[tile], TURNS)
        hidden = jnp.logical_and(shown > turn, turn < TURNS)
        ka[pl.ds(tile * TILE_TOK, TILE_TOK), HD:] = jnp.where(hidden, MASKED, 0.0).astype(BF)
    va[:, HD:] = jnp.ones((SLOTS, HD), BF)
    for part in range(rows // HD):
        turn = lax.broadcasted_iota(jnp.int32, (HD, HD), 0)
        chosen = jnp.where(turn == text_turn[pl.ds(part, 1), :], 1.0, 0.0).T.astype(BF)
        for h in range(heads):
            qa[h, pl.ds(part * HD, HD), HD:] = chosen

    gain_q = q_gain[...]

    def norm_queries(h, carry):
        q_float = q_buf[h].astype(F32)
        inverse = inverse_rms(q_float)
        inv[h] = inverse
        qa[h, :, :HD] = (q_float * inverse * (gain_q * (SCALE * LOG2E))).astype(BF)
        return carry

    for which in range(2):
        for h in range(heads):
            load(h, which).wait()
    lax.fori_loop(0, heads, norm_queries, 0)

    common = NY + NX
    @pl.when(is_owner(z))
    def _():
        pl.semaphore_wait(barrier, common + NZ - 1)

    @pl.when(jnp.logical_not(is_owner(z)))
    def _():
        pl.semaphore_wait(barrier, common + OWNERS)

    scatter = Scatter(scratch[:9], lambda kind, yy: to_c.at[kind, yy], lambda kind, yy: own[kind, yy])
    gather = Gather(scratch[9:13])
    for kind in range(2):
        scatter.start(kind)
    for kind in range(2):
        scatter.over_core(kind)
    for kind in range(2):
        scatter.over_y(kind)

    def key_shard(total):
        raw[...] = total
        gather.over_z(0, total * inverse_rms(total) * k_gain[...])

    scatter.over_z(0, key_shard)
    scatter.over_z(1, lambda total: gather.over_z(1, total))
    for kind in range(2):
        gather.over_y(kind)
    for off in Y_ARRIVAL:
        for kind in range(2):
            gather.over_core(kind, off)
    for off in range(NY):
        for kind in range(2):
            gather.last(kind, off)
    ka[:, :HD] = gather.full[0].reshape(SLOTS, HD)
    va[:, :HD] = gather.full[1].reshape(SLOTS, HD)

    lane = lax.broadcasted_iota(jnp.int32, (rows, HD), 1)
    slot_grad[...] = jnp.zeros_like(slot_grad)

    def forward(h):
        weights = jnp.exp2(rows_dot(qa[h], ka[...])).astype(BF)
        expo[h] = weights
        summed = jnp.dot(weights, va[...], preferred_element_type=F32)
        over = 1.0 / summed[:, HD:]
        att = (summed[:, :HD] * over).astype(BF)
        att_buf[h] = att
        save(h, 0).start()
        up = up_buf[h].astype(F32)
        delta = -jnp.sum(up * att.astype(F32), axis=1, keepdims=True) * over
        high = delta.astype(BF)
        low = (delta - high.astype(F32)).astype(BF)
        up = (up * over).astype(BF)
        da[h, :, :HD] = up
        da[h, :, HD:] = jnp.where(lane == 0, high, jnp.where(lane == 1, low, jnp.zeros_like(low)))
        slot_grad[1] += columns_dot(up, weights)

    def forward_pair(pair, carry):
        forward(2 * pair)
        forward(2 * pair + 1)
        return carry

    lax.fori_loop(0, heads // 2, forward_pair, 0)

    sums = Scatter(
        scratch[13:22], lambda kind, yy: d_kv.at[kind, 1 - core, yy], lambda kind, yy: d_kv[kind, core, yy]
    )
    back = Gather(scratch[22:26])

    def put(kind, factor):
        for cc in range(NC):
            for yy in range(NY):
                d_kv[kind, cc, yy] = (slot_grad[kind, :, pl.ds((cc * NY + yy) * CHUNK, CHUNK)] * factor).T.astype(BF)

    put(1, 1.0)
    sums.start(1)

    def backward(h):
        d_scores = expo[h] * rows_dot(da[h], va[...]).astype(BF)
        expo[h] = d_scores
        slot_grad[0] += columns_dot(qa[h, :, :HD], d_scores)

    def backward_pair(pair, carry):
        backward(2 * pair)
        backward(2 * pair + 1)

        @pl.when(pair == 0)
        def _():
            sums.over_core(1)

        @pl.when(pair == 3)
        def _():
            sums.over_y(1)

        return carry

    lax.fori_loop(0, heads // 2, backward_pair, 0)
    put(0, 1.0 / LOG2E)
    sums.start(0)

    def query_grad(h):
        d_query = jnp.dot(expo[h], ka[:, :HD], preferred_element_type=F32)
        q_float = q_buf[h].astype(F32)
        inverse = inv[h]
        scaled = d_query * (gain_q * SCALE)
        gq_buf[h] = (
            inverse * scaled - q_float * (inverse * inverse * inverse) * jnp.mean(q_float * scaled, axis=1, keepdims=True)
        ).astype(BF)
        save(h, 1).start()

    def query_pair(pair, carry):
        query_grad(2 * pair)
        query_grad(2 * pair + 1)

        @pl.when(pair == 0)
        def _():
            sums.over_core(0)

        @pl.when(pair == 3)
        def _():
            sums.over_y(0)

        return carry

    lax.fori_loop(0, heads // 2, query_pair, 0)

    sums.over_z(1, lambda total: back.over_z(1, total))

    def key_grad_shard(total):
        raw_values = raw[...]
        inverse = inverse_rms(raw_values)
        scaled = total * k_gain[...]
        back.over_z(
            0,
            inverse * scaled
            - raw_values * (inverse * inverse * inverse) * jnp.mean(raw_values * scaled, axis=1, keepdims=True),
        )

    sums.over_z(0, key_grad_shard)
    back.over_y(1)
    back.over_y(0)

    full = back.full

    def to_head(which, off):
        y, z, core = place()
        cc = core if which == 0 else 1 - core
        yy = lax.rem(y + NY - off, NY)
        slot = lax.rem(yy - x + NX + NX - 1, NX)
        return yy != x, remote(
            to_x.at[which, off], from_x.at[cc, slot], sx.at[which, off], rx.at[cc, slot], head=hi * NX + yy
        )

    def vision_term(which, off):
        cc = core if which == 0 else 1 - core
        yy = lax.rem(y + NY - off, NY)
        term = rows_dot(full[0, cc, yy].reshape(CHUNK, HD), w_key[...]) + rows_dot(
            full[1, cc, yy].reshape(CHUNK, HD), w_value[...]
        )
        to_x[which, off] = term.astype(BF)
        other, copy = to_head(which, off)

        @pl.when(other)
        def _():
            copy.start()

    vision_term(0, 0)
    for off in Y_ARRIVAL:
        for kind in (1, 0):
            back.over_core(kind, off)
        vision_term(0, off)
    for off in (0,) + Y_ARRIVAL:
        for kind in (1, 0):
            back.last(kind, off)
        vision_term(1, off)

    def summed_over_x(cc):
        total = to_x[lax.rem(cc + core, NC), lax.rem(y - x + NY, NY)].astype(F32)
        for slot in range(NX - 1):
            remote(
                from_x.at[cc, slot], from_x.at[cc, slot], sx.at[0, slot], rx.at[cc, slot], head=x_peers[0]
            ).wait_recv()
            total = total + from_x[cc, slot].astype(F32)
        return total

    to_hi[...] = summed_over_x(1 - hi).astype(BF)
    over_hi = remote(to_hi, from_hi, sh.at[0], sh.at[1], head=(1 - hi) * NX + x)
    over_hi.start()
    kept = summed_over_x(hi)
    for kind, out in ((0, grad_w_key), (1, grad_w_value)):
        out[...] = columns_dot(vision[...].reshape(SLOTS, vision.shape[-1]), full[kind].reshape(SLOTS, HD))
    scatter.finish()
    gather.finish()
    sums.finish()
    back.finish()
    for which in range(2):
        for h in range(heads):
            save(h, which).wait()
        for off in range(NY):
            other, copy = to_head(which, off)

            @pl.when(other)
            def _(copy=copy):
                copy.wait_send()

    over_hi.wait_recv()
    grad_vision[...] = (kept + from_hi[...].astype(F32)).astype(BF)
    over_hi.wait_send()


def cross(tile_turn, tile_len, query, grad_out, vision, w_key, w_value, text_turn, q_gain, k_gain):
    vmem = pl.BlockSpec(memory_space=pltpu.VMEM)
    smem = pl.BlockSpec(memory_space=pltpu.SMEM)
    hbm = pl.BlockSpec(memory_space=pl.ANY)
    rows, columns = query.shape
    heads = columns // HD
    width = vision.shape[1]
    return pl.pallas_call(
        cross_kernel,
        out_shape=(
            jax.ShapeDtypeStruct(query.shape, BF),
            jax.ShapeDtypeStruct(query.shape, BF),
            jax.ShapeDtypeStruct((CHUNK, width), BF),
            jax.ShapeDtypeStruct((width, HD), F32),
            jax.ShapeDtypeStruct((width, HD), F32),
        ),
        in_specs=[smem, smem, hbm, hbm] + [vmem] * 6,
        out_specs=(hbm, hbm) + (vmem,) * 3,
        scratch_shapes=[
            pltpu.VMEM((heads, rows, HD), BF),
            pltpu.VMEM((heads, rows, HD), BF),
            pltpu.VMEM((heads, rows, HD), BF),
            pltpu.VMEM((heads, rows, HD), BF),
            pltpu.SemaphoreType.DMA((2, heads)),
            pltpu.SemaphoreType.DMA((2, heads)),
            pltpu.VMEM((heads, rows, 2 * HD), BF),
            pltpu.VMEM((heads, rows, 2 * HD), BF),
            pltpu.VMEM((SLOTS, 2 * HD), BF),
            pltpu.VMEM((SLOTS, 2 * HD), BF),
            pltpu.VMEM((heads, rows, 1), F32),
            pltpu.VMEM((heads, rows, SLOTS), BF),
            pltpu.VMEM((2, HD, SLOTS), F32),
            pltpu.VMEM((2, NY, CHUNK, HD), BF),
            pltpu.VMEM((2, NY, CHUNK, HD), F32),
            pltpu.VMEM((SHARD, HD), F32),
            pltpu.VMEM((2, NC, NY, CHUNK, HD), BF),
            pltpu.VMEM((2, NY, CHUNK, width), BF),
            pltpu.VMEM((2, NX, CHUNK, width), BF),
            pltpu.VMEM((CHUNK, width), BF),
            pltpu.VMEM((CHUNK, width), BF),
            pltpu.SemaphoreType.DMA((2, NY)),
            pltpu.SemaphoreType.DMA((2, NX)),
            pltpu.SemaphoreType.DMA((2,)),
        ]
        + (scatter_scratch() + gather_scratch()) * 2,
        compiler_params=pltpu.CompilerParams(collective_id=0, has_side_effects=True, vmem_limit_bytes=VMEM_LIMIT),
        name="cross",
    )(
        tile_turn, tile_len, query, grad_out, vision.reshape(NC, NY, CHUNK, width), w_key, w_value, text_turn, q_gain, k_gain
    )


def emit_kernel(*refs):
    count = len(refs) // 3
    sources, outs, held, sems = refs[:count], refs[count : 2 * count], refs[2 * count : 3 * count], refs[-1]
    pieces = []
    for i in range(count):
        rows = sources[i].shape[0]
        for start in range(0, rows, CHUNK):
            part = pl.ds(start, CHUNK)
            n = len(pieces)
            pieces.append(
                (
                    pltpu.make_async_copy(sources[i].at[part], held[i].at[part], sems.at[0, n]),
                    pltpu.make_async_copy(held[i].at[part], outs[i].at[part], sems.at[1, n]),
                )
            )
    for into, _ in pieces:
        into.start()
    for into, out in pieces:
        into.wait()
        out.start()
    for _, out in pieces:
        out.wait()


def emit(arrays):
    hbm = pl.BlockSpec(memory_space=pl.ANY)
    pieces = sum(a.shape[0] // CHUNK for a in arrays)
    return pl.pallas_call(
        emit_kernel,
        out_shape=tuple(jax.ShapeDtypeStruct(a.shape, a.dtype) for a in arrays),
        in_specs=[hbm] * len(arrays),
        out_specs=(hbm,) * len(arrays),
        scratch_shapes=[pltpu.VMEM(a.shape, a.dtype) for a in arrays] + [pltpu.SemaphoreType.DMA((2, pieces))],
        name="emit",
    )(*arrays)


def body(query, vision, w_key, w_value, q_gain, k_gain, text_turn, tile_turn, tile_len, grad_out):
    outs = cross(
        tile_turn, tile_len, query, grad_out, vision, w_key, w_value,
        text_turn.reshape(-1, HD), q_gain.reshape(1, HD), k_gain.reshape(1, HD),
    )
    return emit(outs)


def solution(mesh):
    return jax.shard_map(
        body,
        mesh=mesh,
        in_specs=(
            P("turn", "head"),
            P(None, "turn"),
            P("turn", "head"),
            P("turn", "head"),
            P(),
            P(),
            P("turn"),
            P(),
            P(),
            P("turn", "head"),
        ),
        out_specs=(
            P("turn", "head"),
            P("turn", "head"),
            P("head", "turn"),
            P("turn", "head"),
            P("turn", "head"),
        ),
        check_vma=False,
    )
```

time: 1940 us -> 90 us (0.05)
  the two profiles are of different devices: /device:TPU:16 before, /device:TPU:3 now
where the time goes in v2:
time: 90 us; the launch traced here: 89.8 us
  Pallas kernels  89.2 us (99%)
    pallas_call x1, Pallas kernels, cross(): pl.pallas_call(cross_kernel, out_shape=(jax.ShapeDtypeStruct(query.shape,...  86.7 us
    pallas_call x1, Pallas kernels, emit(): pl.pallas_call(emit_kernel, out_shape=tuple((jax.ShapeDtypeStruct(a.shape...  2.5 us

profile of v2, /device:TPU:3, one launch (start us, length us, event | category | flops | bytes accessed | tf_op | source)
XLA Modules:
  0.0 89.8 jit_solution(7220225114947439272)
XLA Ops:
  0.6 86.7 %cross.1 = (bf16[512,1024]{1,0:T(8,128)(2,1)}, bf16[512,1024]{1,0:T(8,128)(2,1)}, bf16[128,128]{1,0:T(8,128)(2,1)}, f32[128,128]{1,0:T(8,128)}, f32[128,128]{1,0:T(8,128)}) custom-call(s32[4]{0:T(128)} %tile_turn.1, s32[4]{0:T(128)} %tile_len.1, bf16[512,1024]{1,0:T(8,128)(2,1)} %query.1, bf16[512,1024]{1,0:T(8,128)(2,1)} %grad_out.1, ...), custom_call_target="tpu_custom_call" | custom-call | tf_op jit(solution)/shard_map/cross/pallas_call | solution.py:553
  87.3 2.5 %emit.1 = (bf16[512,1024]{1,0:T(8,128)(2,1)}, bf16[512,1024]{1,0:T(8,128)(2,1)}, bf16[128,128]{1,0:T(8,128)(2,1)}, f32[128,128]{1,0:T(8,128)}, f32[128,128]{1,0:T(8,128)}) custom-call(bf16[512,1024]{1,0:T(8,128)(2,1)} %get-tuple-element.10.refs_0_, bf16[512,1024]{1,0:T(8,128)(2,1)} %get-tuple-element.11.refs_1_, bf16[128,128]{1,0:T(8,128)(2,1)} %get-tuple-element.12.refs_2_, ...), custom_call_target="tpu_custom_call" | custom-call | tf_op jit(solution)/shard_map/emit/pallas_call | solution.py:625

commit v3 on v2

v3 whole, which is shorter than its diff:
```python
import math

import jax
import jax.numpy as jnp
from jax import lax
from jax.experimental import pallas as pl
from jax.experimental.pallas import tpu as pltpu
from jax.sharding import PartitionSpec as P

HD = 128
TILE_TOK = 256
TURNS = 64
EPS = 1e-05

NY, NZ, NC = 4, 8, 2
NHI, NX = 2, 4
CHUNK = 128
OWN_LO, OWNERS = 3, 2
SHARD = CHUNK // OWNERS
SLOTS = NC * NY * CHUNK

BF = jnp.bfloat16
F32 = jnp.float32
MESH = pl.DeviceIdType.MESH
SCALE = 1.0 / math.sqrt(HD)
LOG2E = math.log2(math.e)
MASKED = -16384.0
VMEM_LIMIT = 56 * 1024 * 1024

Y_ORDER = (2, 1, 3)
Y_ARRIVAL = (1, 3, 2)


def place():
    turn = lax.axis_index("turn")
    core = lax.rem(turn, NC)
    z = lax.rem(turn // NC, NZ)
    y = turn // (NC * NZ)
    return y, z, core


def turn_of(y, z, core):
    return (y * NZ + z) * NC + core


def is_owner(z):
    return jnp.logical_and(z >= OWN_LO, z < OWN_LO + OWNERS)


def remote(src, dst, send, recv, **where):
    return pltpu.make_async_remote_copy(
        src_ref=src, dst_ref=dst, send_sem=send, recv_sem=recv, device_id=where, device_id_type=MESH
    )


def scatter_scratch():
    return [
        pltpu.VMEM((2, NY, CHUNK, HD), BF),
        pltpu.VMEM((2, NY, CHUNK, HD), BF),
        pltpu.VMEM((2, NY - 1, CHUNK, HD), BF),
        pltpu.VMEM((2, OWNERS, SHARD, HD), F32),
        pltpu.VMEM((2, OWNERS, SHARD, HD), BF),
        pltpu.VMEM((2, NZ - 1, SHARD, HD), BF),
        pltpu.SemaphoreType.DMA((2, NY)),
        pltpu.SemaphoreType.DMA((2,)),
        pltpu.SemaphoreType.DMA((2,)),
        pltpu.SemaphoreType.DMA((3,)),
    ]


def gather_scratch():
    return [
        pltpu.VMEM((2, NC, NY, OWNERS, SHARD, HD), BF),
        pltpu.SemaphoreType.DMA((2,)),
        pltpu.SemaphoreType.DMA((2, NY)),
        pltpu.SemaphoreType.DMA((2, NY)),
        pltpu.SemaphoreType.DMA((3,)),
    ]


def foreign_scratch():
    return [
        pltpu.VMEM((2, NY, OWNERS, SHARD, HD), BF),
        pltpu.SemaphoreType.DMA((2,)),
        pltpu.SemaphoreType.DMA((2, NY)),
        pltpu.SemaphoreType.DMA((2, NY)),
        pltpu.SemaphoreType.DMA((3,)),
    ]


class Scatter:
    def __init__(self, refs, source, own):
        (self.from_c, self.to_y, self.from_y, self.total, self.to_z, self.from_z, self.rc, self.ry, self.rz, self.sent) = refs
        self.source = source
        self.own = own

    def core_copy(self, kind, off):
        y, z, core = place()
        yy = lax.rem(y + off, NY)
        return remote(
            self.source(kind, yy), self.from_c.at[kind, yy], self.sent.at[0], self.rc.at[kind, off],
            turn=turn_of(y, z, 1 - core),
        )

    def over_core(self, kind):
        y, z, core = place()
        for off in Y_ORDER + (0,):
            yy = lax.rem(y + off, NY)
            self.core_copy(kind, off).wait_recv()
            both = self.own(kind, yy).astype(F32) + self.from_c[kind, yy].astype(F32)
            if off == 0:
                self.total[kind] = both.reshape(OWNERS, SHARD, HD)
            else:
                self.to_y[kind, off] = both.astype(BF)
                remote(
                    self.to_y.at[kind, off], self.from_y.at[kind, off - 1], self.sent.at[1], self.ry.at[kind],
                    turn=turn_of(yy, z, core),
                ).start()

    def wait(self, ref, sem):
        y, z, core = place()
        remote(ref, ref, sem, sem, turn=turn_of(y, z, 1 - core)).wait_recv()

    def wait_sent(self, ref, sem):
        y, z, core = place()
        remote(ref, ref, sem, sem, turn=turn_of(y, z, 1 - core)).wait_send()

    def over_y(self, kind):
        y, z, core = place()
        self.wait(self.from_y.at[kind], self.ry.at[kind])
        total = self.total[kind].reshape(CHUNK, HD)
        for off in range(1, NY):
            total = total + self.from_y[kind, off - 1].astype(F32)
        total = total.reshape(OWNERS, SHARD, HD)
        self.total[kind] = total
        self.to_z[kind] = total.astype(BF)
        far = z // (NZ // 2)
        for step in range(OWNERS):
            owner = (OWNERS - 1 - step) * (1 - far) + step * far

            @pl.when(owner + OWN_LO != z)
            def _(owner=owner):
                slot = lax.rem(z - owner - OWN_LO + NZ + NZ - 1, NZ)
                remote(
                    self.to_z.at[kind, owner], self.from_z.at[kind, slot], self.sent.at[2], self.rz.at[kind],
                    turn=turn_of(y, owner + OWN_LO, core),
                ).start()

    def over_z(self, kind, then):
        y, z, core = place()

        @pl.when(is_owner(z))
        def _():
            total = self.total[kind, z - OWN_LO]
            self.wait(self.from_z.at[kind], self.rz.at[kind])
            for slot in range(NZ - 1):
                total = total + self.from_z[kind, slot].astype(F32)
            then(total)

    def finish(self):
        y, z, core = place()
        self.wait_sent(self.from_c, self.sent.at[0])
        self.wait_sent(self.from_y, self.sent.at[1])

        @pl.when(is_owner(z))
        def _():
            self.wait_sent(self.to_z.at[:, pl.ds(0, OWNERS - 1)], self.sent.at[2])

        @pl.when(jnp.logical_not(is_owner(z)))
        def _():
            self.wait_sent(self.to_z, self.sent.at[2])


class Gather:
    def __init__(self, refs):
        self.full, self.rz, self.ry, self.rc, self.sent = refs

    def chunk(self, kind, cc, yy):
        return self.full.at[kind, cc, yy]

    def over_z(self, kind, shard):
        y, z, core = place()
        self.full[kind, core, y, z - OWN_LO] = shard.astype(BF)
        src = self.full.at[kind, core, y, z - OWN_LO]
        for off in (4, 3, 5, 2, 6, 1, 7):
            remote(src, src, self.sent.at[0], self.rz.at[kind], turn=turn_of(y, lax.rem(z + off, NZ), core)).start()

    def wait(self, ref, sem):
        y, z, core = place()
        remote(ref, ref, sem, sem, turn=turn_of(y, z, 1 - core)).wait_recv()

    def wait_sent(self, ref, sem):
        y, z, core = place()
        remote(ref, ref, sem, sem, turn=turn_of(y, z, 1 - core)).wait_send()

    def over_y(self, kind):
        y, z, core = place()

        @pl.when(is_owner(z))
        def _():
            self.wait(self.full.at[kind, core, y, OWN_LO + OWNERS - 1 - z], self.rz.at[kind])

        @pl.when(jnp.logical_not(is_owner(z)))
        def _():
            self.wait(self.chunk(kind, core, y), self.rz.at[kind])

        self.spread(kind)

    def spread(self, kind):
        y, z, core = place()
        src = self.chunk(kind, core, y)
        for off in Y_ORDER:
            remote(src, src, self.sent.at[1], self.ry.at[kind, off], turn=turn_of(lax.rem(y + off, NY), z, core)).start()
        remote(src, src, self.sent.at[2], self.rc.at[kind, 0], turn=turn_of(y, z, 1 - core)).start()

    def over_core(self, kind, off):
        y, z, core = place()
        chunk = self.chunk(kind, core, lax.rem(y + NY - off, NY))
        self.wait(chunk, self.ry.at[kind, off])
        remote(chunk, chunk, self.sent.at[2], self.rc.at[kind, off], turn=turn_of(y, z, 1 - core)).start()

    def last(self, kind, off):
        y, z, core = place()
        self.wait(self.chunk(kind, 1 - core, lax.rem(y + NY - off, NY)), self.rc.at[kind, off])

    def finish(self, shards, chunks):
        y, z, core = place()

        @pl.when(is_owner(z))
        def _():
            self.wait_sent(shards, self.sent.at[0])

        self.wait_sent(chunks, self.sent.at[1])
        self.wait_sent(self.full.at[:, 0], self.sent.at[2])


class Foreign(Gather):
    def chunk(self, kind, cc, yy):
        return self.full.at[kind, yy]

    def over_z(self, kind, src, head):
        y, z, core = place()
        for zz in range(NZ):
            remote(
                src, self.full.at[kind, y, z - OWN_LO], self.sent.at[0], self.rz.at[kind],
                turn=turn_of(y, zz, core), head=head,
            ).start()

    def over_y(self, kind):
        y, z, core = place()
        self.wait(self.full.at[kind, y], self.rz.at[kind])
        self.spread(kind)


def inverse_rms(values):
    return lax.rsqrt(jnp.mean(values * values, axis=-1, keepdims=True) + EPS)


def rows_dot(a, b):
    return lax.dot_general(a, b, (((1,), (1,)), ((), ())), preferred_element_type=F32)


def columns_dot(a, b):
    return lax.dot_general(a, b, (((0,), (0,)), ((), ())), preferred_element_type=F32)


def cross_kernel(
    tile_turn, tile_len, query, grad_out, vision, w_key, w_value, text_turn, q_gain, k_gain,
    attended, grad_query, grad_vision, grad_w_key, grad_w_value,
    q_buf, up_buf, att_buf, gq_buf, s_io, qa, da, ka, va, inv, expo, slot_grad,
    weights_kv, to_c, own, raw, d_kv, to_x, from_x, far_weights, sx, sw, edge, ready, *scratch
):
    y, z, core = place()
    head = lax.axis_index("head")
    hi, x = head // NX, lax.rem(head, NX)
    rows, heads = q_buf.shape[0], q_buf.shape[1] // HD
    far_head = (1 - hi) * NX + x
    low, high = z == 0, z == NZ - 1
    at_edge = jnp.logical_or(low, high)
    my_edge = (z // (NZ // 2)) * (NZ - 1)

    barrier = pltpu.get_barrier_semaphore()

    def greet(**peer):
        pl.semaphore_signal(barrier, inc=1, device_id=peer, device_id_type=MESH)

    x_peers = [hi * NX + lax.rem(x + off, NX) for off in range(1, NX)]

    @pl.when(at_edge)
    def _():
        greet(turn=turn_of(y, NZ - 1 - z, core), head=far_head)

    @pl.when(jnp.logical_not(at_edge))
    def _():
        greet(turn=turn_of(y, my_edge, core))

    @pl.when(is_owner(z))
    def _():
        for off in range(1, NZ):
            greet(turn=turn_of(y, lax.rem(z + off, NZ), core))

    @pl.when(jnp.logical_not(is_owner(z)))
    def _():
        for owner in range(OWNERS):
            greet(turn=turn_of(y, owner + OWN_LO, core))

    for off in range(1, NY):
        greet(turn=turn_of(lax.rem(y + off, NY), z, core))
    for peer in x_peers:
        greet(head=peer)
    greet(turn=turn_of(y, z, 1 - core))

    load_query = pltpu.make_async_copy(query, q_buf, s_io.at[0])
    load_up = pltpu.make_async_copy(grad_out, up_buf, s_io.at[1])
    save_attended = pltpu.make_async_copy(att_buf, attended, s_io.at[2])
    save_grad = pltpu.make_async_copy(gq_buf, grad_query, s_io.at[3])
    load_query.start()
    load_up.start()

    def columns(h):
        return slice(None), pl.ds(pl.multiple_of(h * HD, HD), HD)

    weights_kv[:, :HD] = w_key[...]
    weights_kv[:, HD:] = w_value[...]

    def project(cc, out):
        both = jnp.dot(vision[cc].reshape(NY * CHUNK, vision.shape[-1]), weights_kv[...], preferred_element_type=F32)
        for kind in range(2):
            out[kind] = both[:, kind * HD : (kind + 1) * HD].reshape(NY, CHUNK, HD).astype(out.dtype)

    project(1 - core, to_c)
    project(core, own)

    for tile in range(SLOTS // TILE_TOK):
        inside = lax.broadcasted_iota(jnp.int32, (TILE_TOK, HD), 0)
        turn = lax.broadcasted_iota(jnp.int32, (TILE_TOK, HD), 1)
        shown = jnp.where(inside < tile_len[tile], tile_turn[tile], TURNS)
        hidden = jnp.logical_and(shown > turn, turn < TURNS)
        ka[pl.ds(tile * TILE_TOK, TILE_TOK), HD:] = jnp.where(hidden, MASKED, 0.0).astype(BF)
    va[:, HD:] = jnp.ones((SLOTS, HD), BF)
    for part in range(rows // HD):
        turn = lax.broadcasted_iota(jnp.int32, (HD, HD), 0)
        chosen = jnp.where(turn == text_turn[pl.ds(part, 1), :], 1.0, 0.0).T.astype(BF)
        for h in range(heads):
            qa[h, pl.ds(part * HD, HD), HD:] = chosen

    gain_q = q_gain[...]

    def norm_queries(h, carry):
        q_float = q_buf[columns(h)].astype(F32)
        inverse = inverse_rms(q_float)
        inv[h] = inverse
        qa[h, :, :HD] = (q_float * inverse * (gain_q * (SCALE * LOG2E))).astype(BF)
        return carry

    common = 1 + (NY - 1) + (NX - 1)
    ends = NZ // 2 - 1 + 1
    owner = is_owner(z)
    for here, count in (
        (owner, NZ - 1),
        (at_edge, OWNERS + ends),
        (jnp.logical_not(jnp.logical_or(owner, at_edge)), OWNERS),
    ):

        @pl.when(here)
        def _(count=count):
            pl.semaphore_wait(barrier, common + count)

    @pl.when(at_edge)
    def _():
        pl.semaphore_signal(
            edge, inc=1, device_id={"turn": turn_of(y, NZ - 1 - z, core), "head": far_head}, device_id_type=MESH
        )

    scatter = Scatter(scratch[:10], lambda kind, yy: to_c.at[kind, yy], lambda kind, yy: own[kind, yy])
    gather = Gather(scratch[10:15])
    for kind in range(2):
        for off in Y_ORDER + (0,):
            scatter.core_copy(kind, off).start()
    for kind in range(2):
        scatter.over_core(kind)
    load_query.wait()
    load_up.wait()
    lax.fori_loop(0, 3, norm_queries, 0)
    for kind in range(2):
        scatter.over_y(kind)
    lax.fori_loop(3, 6, norm_queries, 0)

    def key_shard(total):
        raw[...] = total
        gather.over_z(0, total * inverse_rms(total) * k_gain[...])

    scatter.over_z(0, key_shard)
    scatter.over_z(1, lambda total: gather.over_z(1, total))
    lax.fori_loop(6, heads, norm_queries, 0)
    for kind in range(2):
        gather.over_y(kind)
    for off in Y_ARRIVAL:
        for kind in range(2):
            gather.over_core(kind, off)
    for off in range(NY):
        for kind in range(2):
            gather.last(kind, off)

    @pl.when(at_edge)
    def _():
        pl.semaphore_wait(edge, 1)
        pl.semaphore_signal(ready, inc=1)
        for off in range(1, NZ):
            pl.semaphore_signal(
                ready, inc=1, device_id={"turn": turn_of(y, lax.rem(z + off, NZ), core)}, device_id_type=MESH
            )

    ka[:, :HD] = gather.full[0].reshape(SLOTS, HD)
    va[:, :HD] = gather.full[1].reshape(SLOTS, HD)

    lane = lax.broadcasted_iota(jnp.int32, (rows, HD), 1)
    slot_grad[...] = jnp.zeros_like(slot_grad)

    def forward(h):
        weights = jnp.exp2(rows_dot(qa[h], ka[...])).astype(BF)
        expo[h] = weights
        summed = jnp.dot(weights, va[...], preferred_element_type=F32)
        over = 1.0 / summed[:, HD:]
        att = (summed[:, :HD] * over).astype(BF)
        att_buf[columns(h)] = att
        up = up_buf[columns(h)].astype(F32)
        delta = -jnp.sum(up * att.astype(F32), axis=1, keepdims=True) * over
        high = delta.astype(BF)
        low = (delta - high.astype(F32)).astype(BF)
        up = (up * over).astype(BF)
        da[h, :, :HD] = up
        da[h, :, HD:] = jnp.where(lane == 0, high, jnp.where(lane == 1, low, jnp.zeros_like(low)))
        slot_grad[1] += columns_dot(up, weights)

    def forward_pair(pair, carry):
        for one in range(4):
            forward(4 * pair + one)
        return carry

    lax.fori_loop(0, heads // 4, forward_pair, 0)

    save_attended.start()
    sums = Scatter(
        scratch[15:25], lambda kind, yy: d_kv.at[kind, 1 - core, yy], lambda kind, yy: d_kv[kind, core, yy]
    )
    back = Gather(scratch[25:30])
    far = Foreign(scratch[30:35])

    def put(kind, factor):
        for cc in (1 - core, core):
            for off in Y_ORDER + (0,):
                yy = lax.rem(y + off, NY)
                start = pl.multiple_of((cc * NY + yy) * CHUNK, CHUNK)
                d_kv[kind, cc, yy] = (slot_grad[kind, :, pl.ds(start, CHUNK)] * factor).T.astype(BF)
                if cc is not core:
                    sums.core_copy(kind, off).start()

    put(1, 1.0)
    pl.semaphore_wait(ready, 2)
    for kind, weight in enumerate((w_key, w_value)):
        remote(weight, far_weights.at[kind], sw.at[0], sw.at[1], head=far_head).start()

    def backward(h):
        d_scores = expo[h] * rows_dot(da[h], va[...]).astype(BF)
        expo[h] = d_scores
        slot_grad[0] += columns_dot(qa[h, :, :HD], d_scores)

    def backward_pair(pair, carry):
        for one in range(4):
            backward(4 * pair + one)

        @pl.when(pair == 0)
        def _():
            sums.over_core(1)

        @pl.when(pair == 1)
        def _():
            sums.over_y(1)

        return carry

    lax.fori_loop(0, heads // 4, backward_pair, 0)
    put(0, 1.0 / LOG2E)

    def query_grad(h):
        d_query = jnp.dot(expo[h], ka[:, :HD], preferred_element_type=F32)
        q_float = q_buf[columns(h)].astype(F32)
        inverse = inv[h]
        scaled = d_query * (gain_q * SCALE)
        gq_buf[columns(h)] = (
            inverse * scaled - q_float * (inverse * inverse * inverse) * jnp.mean(q_float * scaled, axis=1, keepdims=True)
        ).astype(BF)

    def query_pair(pair, carry):
        query_grad(2 * pair)
        query_grad(2 * pair + 1)

        @pl.when(pair == 0)
        def _():
            sums.over_core(0)

        @pl.when(pair == 3)
        def _():
            sums.over_y(0)

        return carry

    lax.fori_loop(0, heads // 2, query_pair, 0)

    save_grad.start()

    def spread(kind, total):
        back.over_z(kind, total)

        @pl.when(core != hi)
        def _():
            far.over_z(kind, back.full.at[kind, core, y, z - OWN_LO], far_head)

    def key_grad_shard(total):
        raw_values = raw[...]
        inverse = inverse_rms(raw_values)
        scaled = total * k_gain[...]
        spread(
            0,
            inverse * scaled
            - raw_values * (inverse * inverse * inverse) * jnp.mean(raw_values * scaled, axis=1, keepdims=True),
        )

    sums.over_z(1, lambda total: spread(1, total))
    sums.over_z(0, key_grad_shard)
    direct, relayed = core == hi, core != hi

    def far_over_y(kind):
        @pl.when(direct)
        def _():
            far.over_y(kind)

    back.over_y(1)
    far_over_y(1)
    back.over_y(0)
    far_over_y(0)

    remote(far_weights, far_weights, sw.at[0], sw.at[1], head=far_head).wait_recv()

    def vision_term(off):
        yy = lax.rem(y + NY - off, NY)
        terms = [
            rows_dot(values.reshape(CHUNK, HD), weight)
            for values, weight in (
                (back.full[1, hi, yy], w_value[...]),
                (far.full[1, yy], far_weights[1]),
                (back.full[0, hi, yy], w_key[...]),
                (far.full[0, yy], far_weights[0]),
            )
        ]
        to_x[off] = (terms[0] + terms[1] + terms[2] + terms[3]).astype(BF)

        @pl.when(yy != x)
        def _():
            slot = lax.rem(yy - x + NX + NX - 1, NX)
            remote(to_x.at[off], from_x.at[slot], sx.at[0], sx.at[1], head=hi * NX + yy).start()

    for off in (0,) + Y_ARRIVAL:
        if off:
            for kind in (1, 0):
                back.over_core(kind, off)

        @pl.when(direct)
        def _(off=off):
            if off:
                for kind in (1, 0):
                    far.over_core(kind, off)
            vision_term(off)

    for off in (0,) + Y_ARRIVAL:
        for kind in (1, 0):
            back.last(kind, off)

        @pl.when(relayed)
        def _(off=off):
            for kind in (1, 0):
                far.last(kind, off)
            vision_term(off)

    for kind, out in ((0, grad_w_key), (1, grad_w_value)):
        out[...] = columns_dot(vision[...].reshape(SLOTS, vision.shape[-1]), back.full[kind].reshape(SLOTS, HD))
    total = to_x[lax.rem(y - x + NY, NY)].astype(F32)
    landed = from_x.at[pl.ds(0, NX - 1)]
    remote(landed, landed, sx.at[0], sx.at[1], head=x_peers[0]).wait_recv()
    for slot in range(NX - 1):
        total = total + from_x[slot].astype(F32)
    grad_vision[...] = total.astype(BF)

    remote(landed, landed, sx.at[0], sx.at[1], head=x_peers[0]).wait_send()
    remote(far_weights, far_weights, sw.at[0], sw.at[1], head=far_head).wait_send()
    scatter.finish()
    sums.finish()
    gather.finish(sums.from_z, sums.from_y)
    back.finish(sums.from_z, sums.from_y)

    @pl.when(direct)
    def _():
        far.wait_sent(sums.from_y, far.sent.at[1])
        far.wait_sent(far.full, far.sent.at[2])

    @pl.when(jnp.logical_and(relayed, is_owner(z)))
    def _():
        far.wait_sent(back.full.at[:, 0], far.sent.at[0])

    save_attended.wait()
    save_grad.wait()


def cross(tile_turn, tile_len, query, grad_out, vision, w_key, w_value, text_turn, q_gain, k_gain):
    vmem = pl.BlockSpec(memory_space=pltpu.VMEM)
    smem = pl.BlockSpec(memory_space=pltpu.SMEM)
    hbm = pl.BlockSpec(memory_space=pl.ANY)
    rows, columns = query.shape
    heads = columns // HD
    width = vision.shape[1]
    return pl.pallas_call(
        cross_kernel,
        out_shape=(
            jax.ShapeDtypeStruct(query.shape, BF),
            jax.ShapeDtypeStruct(query.shape, BF),
            jax.ShapeDtypeStruct((CHUNK, width), BF),
            jax.ShapeDtypeStruct((width, HD), F32),
            jax.ShapeDtypeStruct((width, HD), F32),
        ),
        in_specs=[smem, smem, hbm, hbm] + [vmem] * 6,
        out_specs=(hbm, hbm) + (vmem,) * 3,
        scratch_shapes=[
            pltpu.VMEM((rows, columns), BF),
            pltpu.VMEM((rows, columns), BF),
            pltpu.VMEM((rows, columns), BF),
            pltpu.VMEM((rows, columns), BF),
            pltpu.SemaphoreType.DMA((4,)),
            pltpu.VMEM((heads, rows, 2 * HD), BF),
            pltpu.VMEM((heads, rows, 2 * HD), BF),
            pltpu.VMEM((SLOTS, 2 * HD), BF),
            pltpu.VMEM((SLOTS, 2 * HD), BF),
            pltpu.VMEM((heads, rows, 1), F32),
            pltpu.VMEM((heads, rows, SLOTS), BF),
            pltpu.VMEM((2, HD, SLOTS), F32),
            pltpu.VMEM((HD, 2 * HD), BF),
            pltpu.VMEM((2, NY, CHUNK, HD), BF),
            pltpu.VMEM((2, NY, CHUNK, HD), F32),
            pltpu.VMEM((SHARD, HD), F32),
            pltpu.VMEM((2, NC, NY, CHUNK, HD), BF),
            pltpu.VMEM((NY, CHUNK, width), BF),
            pltpu.VMEM((NX, CHUNK, width), BF),
            pltpu.VMEM((2, width, HD), BF),
            pltpu.SemaphoreType.DMA((2,)),
            pltpu.SemaphoreType.DMA((2,)),
            pltpu.SemaphoreType.REGULAR,
            pltpu.SemaphoreType.REGULAR,
        ]
        + (scatter_scratch() + gather_scratch()) * 2
        + foreign_scratch(),
        compiler_params=pltpu.CompilerParams(collective_id=0, has_side_effects=True, vmem_limit_bytes=VMEM_LIMIT),
        name="cross",
    )(
        tile_turn, tile_len, query, grad_out, vision.reshape(NC, NY, CHUNK, width), w_key, w_value, text_turn, q_gain, k_gain
    )


def emit_kernel(*refs):
    count = len(refs) // 3
    sources, outs, held, sems = refs[:count], refs[count : 2 * count], refs[2 * count : 3 * count], refs[-1]
    pieces = []
    for i in range(count):
        rows = sources[i].shape[0]
        for start in range(0, rows, CHUNK):
            part = pl.ds(start, CHUNK)
            n = len(pieces)
            pieces.append(
                (
                    pltpu.make_async_copy(sources[i].at[part], held[i].at[part], sems.at[0, n]),
                    pltpu.make_async_copy(held[i].at[part], outs[i].at[part], sems.at[1, n]),
                )
            )
    for into, _ in pieces:
        into.start()
    for into, out in pieces:
        into.wait()
        out.start()
    for _, out in pieces:
        out.wait()


def emit(arrays):
    hbm = pl.BlockSpec(memory_space=pl.ANY)
    pieces = sum(a.shape[0] // CHUNK for a in arrays)
    return pl.pallas_call(
        emit_kernel,
        out_shape=tuple(jax.ShapeDtypeStruct(a.shape, a.dtype) for a in arrays),
        in_specs=[hbm] * len(arrays),
        out_specs=(hbm,) * len(arrays),
        scratch_shapes=[pltpu.VMEM(a.shape, a.dtype) for a in arrays] + [pltpu.SemaphoreType.DMA((2, pieces))],
        name="emit",
    )(*arrays)


def body(query, vision, w_key, w_value, q_gain, k_gain, text_turn, tile_turn, tile_len, grad_out):
    outs = cross(
        tile_turn, tile_len, query, grad_out, vision, w_key, w_value,
        text_turn.reshape(-1, HD), q_gain.reshape(1, HD), k_gain.reshape(1, HD),
    )
    return emit(outs)


def solution(mesh):
    return jax.shard_map(
        body,
        mesh=mesh,
        in_specs=(
            P("turn", "head"),
            P(None, "turn"),
            P("turn", "head"),
            P("turn", "head"),
            P(),
            P(),
            P("turn"),
            P(),
            P(),
            P("turn", "head"),
        ),
        out_specs=(
            P("turn", "head"),
            P("turn", "head"),
            P("head", "turn"),
            P("turn", "head"),
            P("turn", "head"),
        ),
        check_vma=False,
    )
```

time: 90 us -> 82.2 us (0.913)
  the two profiles are of different devices: /device:TPU:3 before, /device:TPU:9 now
where the time goes in v3:
time: 82.2 us; the launch traced here: 82 us
  Pallas kernels  81.4 us (99%)
    pallas_call x1, Pallas kernels, cross(): pl.pallas_call(cross_kernel, out_shape=(jax.ShapeDtypeStruct(query.shape,...  78.9 us
    pallas_call x1, Pallas kernels, emit(): pl.pallas_call(emit_kernel, out_shape=tuple((jax.ShapeDtypeStruct(a.shape...  2.5 us

profile of v3, /device:TPU:9, one launch (start us, length us, event | category | flops | bytes accessed | tf_op | source)
XLA Modules:
  0.0 82.0 jit_solution(573116289257295241)
XLA Ops:
  0.6 78.9 %cross.1 = (bf16[512,1024]{1,0:T(8,128)(2,1)}, bf16[512,1024]{1,0:T(8,128)(2,1)}, bf16[128,128]{1,0:T(8,128)(2,1)}, f32[128,128]{1,0:T(8,128)}, f32[128,128]{1,0:T(8,128)}) custom-call(s32[4]{0:T(128)} %tile_turn.1, s32[4]{0:T(128)} %tile_len.1, bf16[512,1024]{1,0:T(8,128)(2,1)} %query.1, bf16[512,1024]{1,0:T(8,128)(2,1)} %grad_out.1, ...), custom_call_target="tpu_custom_call" | custom-call | tf_op jit(solution)/shard_map/cross/pallas_call | solution.py:622
  79.5 2.5 %emit.1 = (bf16[512,1024]{1,0:T(8,128)(2,1)}, bf16[512,1024]{1,0:T(8,128)(2,1)}, bf16[128,128]{1,0:T(8,128)(2,1)}, f32[128,128]{1,0:T(8,128)}, f32[128,128]{1,0:T(8,128)}) custom-call(bf16[512,1024]{1,0:T(8,128)(2,1)} %get-tuple-element.10.refs_0_, bf16[512,1024]{1,0:T(8,128)(2,1)} %get-tuple-element.11.refs_1_, bf16[128,128]{1,0:T(8,128)(2,1)} %get-tuple-element.12.refs_2_, ...), custom_call_target="tpu_custom_call" | custom-call | tf_op jit(solution)/shard_map/emit/pallas_call | solution.py:695

commit v4 on v3

--- a/solution.py
+++ b/solution.py
@@ -25,7 +25,7 @@
 SCALE = 1.0 / math.sqrt(HD)
 LOG2E = math.log2(math.e)
 MASKED = -16384.0
-VMEM_LIMIT = 56 * 1024 * 1024
+VMEM_LIMIT = 40 * 1024 * 1024
 
 Y_ORDER = (2, 1, 3)
 Y_ARRIVAL = (1, 3, 2)
@@ -83,8 +83,7 @@
         pltpu.VMEM((2, NY, OWNERS, SHARD, HD), BF),
         pltpu.SemaphoreType.DMA((2,)),
         pltpu.SemaphoreType.DMA((2, NY)),
-        pltpu.SemaphoreType.DMA((2, NY)),
-        pltpu.SemaphoreType.DMA((3,)),
+        pltpu.SemaphoreType.DMA((2,)),
     ]
 
 
@@ -206,11 +205,16 @@
 
         self.spread(kind)
 
-    def spread(self, kind):
+    def spread_y(self, kind):
         y, z, core = place()
         src = self.chunk(kind, core, y)
         for off in Y_ORDER:
             remote(src, src, self.sent.at[1], self.ry.at[kind, off], turn=turn_of(lax.rem(y + off, NY), z, core)).start()
+
+    def spread(self, kind):
+        y, z, core = place()
+        self.spread_y(kind)
+        src = self.chunk(kind, core, y)
         remote(src, src, self.sent.at[2], self.rc.at[kind, 0], turn=turn_of(y, z, 1 - core)).start()
 
     def over_core(self, kind, off):
@@ -235,6 +239,9 @@
 
 
 class Foreign(Gather):
+    def __init__(self, refs):
+        self.full, self.rz, self.ry, self.sent = refs
+
     def chunk(self, kind, cc, yy):
         return self.full.at[kind, yy]
 
@@ -249,7 +256,11 @@
     def over_y(self, kind):
         y, z, core = place()
         self.wait(self.full.at[kind, y], self.rz.at[kind])
-        self.spread(kind)
+        self.spread_y(kind)
+
+    def arrived(self, kind, off):
+        y, z, core = place()
+        self.wait(self.chunk(kind, core, lax.rem(y + NY - off, NY)), self.ry.at[kind, off])
 
 
 def inverse_rms(values):
@@ -265,10 +276,10 @@
 
 
 def cross_kernel(
-    tile_turn, tile_len, query, grad_out, vision, w_key, w_value, text_turn, q_gain, k_gain,
-    attended, grad_query, grad_vision, grad_w_key, grad_w_value,
-    q_buf, up_buf, att_buf, gq_buf, s_io, qa, da, ka, va, inv, expo, slot_grad,
-    weights_kv, to_c, own, raw, d_kv, to_x, from_x, far_weights, sx, sw, edge, ready, *scratch
+    tile_turn_in, tile_len_in, query, grad_out, vision_in, w_key_in, w_value_in, text_turn_in, q_gain_in, k_gain_in,
+    att_buf, gq_buf, grad_vision, grad_w_key, grad_w_value,
+    q_buf, up_buf, vision, w_key, w_value, text_turn, q_gain, k_gain, tile_turn, tile_len, s_io, qa, da, ka, va, inv, expo, slot_grad,
+    weights_kv, vision_t, v_terms, to_c, own, raw, d_kv, to_x, from_x, near_weights, far_weights, sx, sn, sw, edge, beside, ready, *scratch
 ):
     y, z, core = place()
     head = lax.axis_index("head")
@@ -306,20 +317,31 @@
 
     for off in range(1, NY):
         greet(turn=turn_of(lax.rem(y + off, NY), z, core))
-    for peer in x_peers:
-        greet(head=peer)
+
+    @pl.when(z == OWN_LO)
+    def _():
+        for peer in x_peers:
+            greet(head=peer)
+
     greet(turn=turn_of(y, z, 1 - core))
 
-    load_query = pltpu.make_async_copy(query, q_buf, s_io.at[0])
-    load_up = pltpu.make_async_copy(grad_out, up_buf, s_io.at[1])
-    save_attended = pltpu.make_async_copy(att_buf, attended, s_io.at[2])
-    save_grad = pltpu.make_async_copy(gq_buf, grad_query, s_io.at[3])
-    load_query.start()
-    load_up.start()
+    loads = [
+        pltpu.make_async_copy(src, dst, s_io.at[n])
+        for n, (src, dst) in enumerate(
+            (
+                (vision_in, vision), (w_key_in, w_key), (w_value_in, w_value), (tile_turn_in, tile_turn), (tile_len_in, tile_len),
+                (text_turn_in, text_turn), (q_gain_in, q_gain), (k_gain_in, k_gain), (query, q_buf), (grad_out, up_buf),
+            )
+        )
+    ]
+    for load in loads:
+        load.start()
 
     def columns(h):
         return slice(None), pl.ds(pl.multiple_of(h * HD, HD), HD)
 
+    for load in loads[:3]:
+        load.wait()
     weights_kv[:, :HD] = w_key[...]
     weights_kv[:, HD:] = w_value[...]
 
@@ -331,6 +353,50 @@
     project(1 - core, to_c)
     project(core, own)
 
+    def norm_queries(h, carry):
+        gain_q = q_gain[...]
+        q_float = q_buf[columns(h)].astype(F32)
+        inverse = inverse_rms(q_float)
+        inv[h] = inverse
+        qa[h, :, :HD] = (q_float * inverse * (gain_q * (SCALE * LOG2E))).astype(BF)
+        return carry
+
+    common = 1 + (NY - 1)
+    ends = NZ // 2 - 1 + 1
+    owner = is_owner(z)
+    for here, count in (
+        (z == OWN_LO, NZ - 1 + NX - 1),
+        (jnp.logical_and(owner, z != OWN_LO), NZ - 1),
+        (at_edge, OWNERS + ends),
+        (jnp.logical_not(jnp.logical_or(owner, at_edge)), OWNERS),
+    ):
+
+        @pl.when(here)
+        def _(count=count):
+            pl.semaphore_wait(barrier, common + count)
+
+    @pl.when(at_edge)
+    def _():
+        pl.semaphore_signal(
+            edge, inc=1, device_id={"turn": turn_of(y, NZ - 1 - z, core), "head": far_head}, device_id_type=MESH
+        )
+
+    @pl.when(z == OWN_LO)
+    def _():
+        for peer in x_peers:
+            pl.semaphore_signal(beside, inc=1, device_id={"head": peer}, device_id_type=MESH)
+
+    scatter = Scatter(scratch[:10], lambda kind, yy: to_c.at[kind, yy], lambda kind, yy: own[kind, yy])
+    gather = Gather(scratch[10:15])
+    for kind in range(2):
+        for off in Y_ORDER + (0,):
+            scatter.core_copy(kind, off).start()
+    for kind, weight in enumerate((w_key, w_value)):
+        near_weights[kind, 0] = weight[...]
+        remote(weight, near_weights.at[kind, 1], sn.at[0], sn.at[1], turn=turn_of(y, z, 1 - core)).start()
+    scatter.over_core(0)
+    for load in loads[3:]:
+        load.wait()
     for tile in range(SLOTS // TILE_TOK):
         inside = lax.broadcasted_iota(jnp.int32, (TILE_TOK, HD), 0)
         turn = lax.broadcasted_iota(jnp.int32, (TILE_TOK, HD), 1)
@@ -338,88 +404,74 @@
         hidden = jnp.logical_and(shown > turn, turn < TURNS)
         ka[pl.ds(tile * TILE_TOK, TILE_TOK), HD:] = jnp.where(hidden, MASKED, 0.0).astype(BF)
     va[:, HD:] = jnp.ones((SLOTS, HD), BF)
+    vision_t[...] = vision[...].reshape(SLOTS, vision.shape[-1]).T
     for part in range(rows // HD):
         turn = lax.broadcasted_iota(jnp.int32, (HD, HD), 0)
         chosen = jnp.where(turn == text_turn[pl.ds(part, 1), :], 1.0, 0.0).T.astype(BF)
         for h in range(heads):
             qa[h, pl.ds(part * HD, HD), HD:] = chosen
 
-    gain_q = q_gain[...]
-
-    def norm_queries(h, carry):
-        q_float = q_buf[columns(h)].astype(F32)
-        inverse = inverse_rms(q_float)
-        inv[h] = inverse
-        qa[h, :, :HD] = (q_float * inverse * (gain_q * (SCALE * LOG2E))).astype(BF)
-        return carry
-
-    common = 1 + (NY - 1) + (NX - 1)
-    ends = NZ // 2 - 1 + 1
-    owner = is_owner(z)
-    for here, count in (
-        (owner, NZ - 1),
-        (at_edge, OWNERS + ends),
-        (jnp.logical_not(jnp.logical_or(owner, at_edge)), OWNERS),
-    ):
-
-        @pl.when(here)
-        def _(count=count):
-            pl.semaphore_wait(barrier, common + count)
-
-    @pl.when(at_edge)
-    def _():
-        pl.semaphore_signal(
-            edge, inc=1, device_id={"turn": turn_of(y, NZ - 1 - z, core), "head": far_head}, device_id_type=MESH
-        )
-
-    scatter = Scatter(scratch[:10], lambda kind, yy: to_c.at[kind, yy], lambda kind, yy: own[kind, yy])
-    gather = Gather(scratch[10:15])
-    for kind in range(2):
-        for off in Y_ORDER + (0,):
-            scatter.core_copy(kind, off).start()
-    for kind in range(2):
-        scatter.over_core(kind)
-    load_query.wait()
-    load_up.wait()
     lax.fori_loop(0, 3, norm_queries, 0)
-    for kind in range(2):
-        scatter.over_y(kind)
-    lax.fori_loop(3, 6, norm_queries, 0)
+    scatter.over_y(0)
+    scatter.over_core(1)
+    lax.fori_loop(3, heads, norm_queries, 0)
 
     def key_shard(total):
         raw[...] = total
         gather.over_z(0, total * inverse_rms(total) * k_gain[...])
 
     scatter.over_z(0, key_shard)
+    scatter.over_y(1)
+    gather.over_y(0)
     scatter.over_z(1, lambda total: gather.over_z(1, total))
-    lax.fori_loop(6, heads, norm_queries, 0)
-    for kind in range(2):
-        gather.over_y(kind)
     for off in Y_ARRIVAL:
-        for kind in range(2):
-            gather.over_core(kind, off)
+        gather.over_core(0, off)
+    gather.over_y(1)
     for off in range(NY):
-        for kind in range(2):
-            gather.last(kind, off)
+        gather.last(0, off)
+    ka[:, :HD] = gather.full[0].reshape(SLOTS, HD)
+
+    def score(h):
+        expo[h] = jnp.exp2(rows_dot(qa[h], ka[...])).astype(BF)
+
+    def score_pair(pair, carry):
+        score(2 * pair)
+        score(2 * pair + 1)
+
+        @pl.when(pair == 1)
+        def _():
+            for off in Y_ARRIVAL:
+                gather.over_core(1, off)
+
+        return carry
+
+    lax.fori_loop(0, heads // 2, score_pair, 0)
+    for off in range(NY):
+        gather.last(1, off)
+
+    @pl.when(z == OWN_LO)
+    def _():
+        pl.semaphore_wait(beside, NX - 1)
 
     @pl.when(at_edge)
     def _():
         pl.semaphore_wait(edge, 1)
+
+    @pl.when(jnp.logical_or(z == OWN_LO, at_edge))
+    def _():
         pl.semaphore_signal(ready, inc=1)
         for off in range(1, NZ):
             pl.semaphore_signal(
                 ready, inc=1, device_id={"turn": turn_of(y, lax.rem(z + off, NZ), core)}, device_id_type=MESH
             )
 
-    ka[:, :HD] = gather.full[0].reshape(SLOTS, HD)
     va[:, :HD] = gather.full[1].reshape(SLOTS, HD)
 
     lane = lax.broadcasted_iota(jnp.int32, (rows, HD), 1)
     slot_grad[...] = jnp.zeros_like(slot_grad)
 
     def forward(h):
-        weights = jnp.exp2(rows_dot(qa[h], ka[...])).astype(BF)
-        expo[h] = weights
+        weights = expo[h]
         summed = jnp.dot(weights, va[...], preferred_element_type=F32)
         over = 1.0 / summed[:, HD:]
         att = (summed[:, :HD] * over).astype(BF)
@@ -440,7 +492,6 @@
 
     lax.fori_loop(0, heads // 4, forward_pair, 0)
 
-    save_attended.start()
     sums = Scatter(
         scratch[15:25], lambda kind, yy: d_kv.at[kind, 1 - core, yy], lambda kind, yy: d_kv[kind, core, yy]
     )
@@ -457,9 +508,16 @@
                     sums.core_copy(kind, off).start()
 
     put(1, 1.0)
-    pl.semaphore_wait(ready, 2)
-    for kind, weight in enumerate((w_key, w_value)):
-        remote(weight, far_weights.at[kind], sw.at[0], sw.at[1], head=far_head).start()
+    pl.semaphore_wait(ready, 3)
+    from_core = near_weights.at[:, 1]
+    remote(from_core, from_core, sn.at[0], sn.at[1], turn=turn_of(y, z, 1 - core)).wait()
+
+    direct, relayed = core == hi, core != hi
+
+    @pl.when(relayed)
+    def _():
+        for kind in range(2):
+            remote(near_weights.at[kind], far_weights.at[kind], sw.at[0], sw.at[1], head=far_head).start()
 
     def backward(h):
         d_scores = expo[h] * rows_dot(da[h], va[...]).astype(BF)
@@ -467,27 +525,34 @@
         slot_grad[0] += columns_dot(qa[h, :, :HD], d_scores)
 
     def backward_pair(pair, carry):
-        for one in range(4):
-            backward(4 * pair + one)
+        backward(2 * pair)
+        backward(2 * pair + 1)
 
         @pl.when(pair == 0)
         def _():
             sums.over_core(1)
 
-        @pl.when(pair == 1)
+        @pl.when(pair == 3)
         def _():
             sums.over_y(1)
 
         return carry
 
-    lax.fori_loop(0, heads // 4, backward_pair, 0)
+    lax.fori_loop(0, heads // 2, backward_pair, 0)
     put(0, 1.0 / LOG2E)
+
+    def spread(kind, total):
+        back.over_z(kind, total)
+
+        @pl.when(core != hi)
+        def _():
+            far.over_z(kind, back.full.at[kind, core, y, z - OWN_LO], far_head)
 
     def query_grad(h):
         d_query = jnp.dot(expo[h], ka[:, :HD], preferred_element_type=F32)
         q_float = q_buf[columns(h)].astype(F32)
         inverse = inv[h]
-        scaled = d_query * (gain_q * SCALE)
+        scaled = d_query * (q_gain[...] * SCALE)
         gq_buf[columns(h)] = (
             inverse * scaled - q_float * (inverse * inverse * inverse) * jnp.mean(q_float * scaled, axis=1, keepdims=True)
         ).astype(BF)
@@ -500,6 +565,10 @@
         def _():
             sums.over_core(0)
 
+        @pl.when(pair == 2)
+        def _():
+            sums.over_z(1, lambda total: spread(1, total))
+
         @pl.when(pair == 3)
         def _():
             sums.over_y(0)
@@ -508,14 +577,6 @@
 
     lax.fori_loop(0, heads // 2, query_pair, 0)
 
-    save_grad.start()
-
-    def spread(kind, total):
-        back.over_z(kind, total)
-
-        @pl.when(core != hi)
-        def _():
-            far.over_z(kind, back.full.at[kind, core, y, z - OWN_LO], far_head)
 
     def key_grad_shard(total):
         raw_values = raw[...]
@@ -527,73 +588,73 @@
             - raw_values * (inverse * inverse * inverse) * jnp.mean(raw_values * scaled, axis=1, keepdims=True),
         )
 
-    sums.over_z(1, lambda total: spread(1, total))
     sums.over_z(0, key_grad_shard)
-    direct, relayed = core == hi, core != hi
-
     def far_over_y(kind):
         @pl.when(direct)
         def _():
             far.over_y(kind)
+
+    def vision_term(kind, off):
+        yy = lax.rem(y + NY - off, NY)
+        return rows_dot(
+            back.full[kind, hi, yy].reshape(CHUNK, HD), near_weights[kind].reshape(NC * CHUNK, HD)
+        ) + rows_dot(far.full[kind, yy].reshape(CHUNK, HD), far_weights[kind].reshape(NC * CHUNK, HD))
+
+    def send_terms(off):
+        yy = lax.rem(y + NY - off, NY)
+        both = v_terms[off] + vision_term(0, off)
+        slot = lax.rem(yy - x + NX + NX - 1, NX)
+        width = vision.shape[-1]
+        to_x[NC * off] = both[:, :width].astype(BF)
+        to_x[NC * off + 1] = both[:, width:].astype(BF)
+        remote(
+            to_x.at[NC * off + 1], from_x.at[slot], sx.at[0], sx.at[1], turn=turn_of(y, z, 1 - core), head=hi * NX + yy
+        ).start()
+
+        @pl.when(yy != x)
+        def _():
+            remote(to_x.at[NC * off], from_x.at[slot], sx.at[0], sx.at[1], head=hi * NX + yy).start()
+
+    def weight_grad(kind, out):
+        out[...] = jnp.dot(vision_t[...], back.full[kind].reshape(SLOTS, HD), preferred_element_type=F32)
 
     back.over_y(1)
     far_over_y(1)
     back.over_y(0)
+    for off in Y_ARRIVAL:
+        back.over_core(1, off)
+
+    @pl.when(direct)
+    def _():
+        remote(far_weights, far_weights, sw.at[0], sw.at[1], head=far_head).wait_recv()
+        for off in Y_ARRIVAL:
+            far.arrived(1, off)
+
     far_over_y(0)
 
-    remote(far_weights, far_weights, sw.at[0], sw.at[1], head=far_head).wait_recv()
-
-    def vision_term(off):
-        yy = lax.rem(y + NY - off, NY)
-        terms = [
-            rows_dot(values.reshape(CHUNK, HD), weight)
-            for values, weight in (
-                (back.full[1, hi, yy], w_value[...]),
-                (far.full[1, yy], far_weights[1]),
-                (back.full[0, hi, yy], w_key[...]),
-                (far.full[0, yy], far_weights[0]),
-            )
-        ]
-        to_x[off] = (terms[0] + terms[1] + terms[2] + terms[3]).astype(BF)
-
-        @pl.when(yy != x)
-        def _():
-            slot = lax.rem(yy - x + NX + NX - 1, NX)
-            remote(to_x.at[off], from_x.at[slot], sx.at[0], sx.at[1], head=hi * NX + yy).start()
+    @pl.when(direct)
+    def _():
+        for off in range(NY):
+            v_terms[off] = vision_term(1, off)
+
+    for off in range(NY):
+        back.last(1, off)
+    weight_grad(1, grad_w_value)
 
     for off in (0,) + Y_ARRIVAL:
         if off:
-            for kind in (1, 0):
-                back.over_core(kind, off)
+            back.over_core(0, off)
 
         @pl.when(direct)
         def _(off=off):
             if off:
-                for kind in (1, 0):
-                    far.over_core(kind, off)
-            vision_term(off)
-
-    for off in (0,) + Y_ARRIVAL:
-        for kind in (1, 0):
-            back.last(kind, off)
-
-        @pl.when(relayed)
-        def _(off=off):
-            for kind in (1, 0):
-                far.last(kind, off)
-            vision_term(off)
-
-    for kind, out in ((0, grad_w_key), (1, grad_w_value)):
-        out[...] = columns_dot(vision[...].reshape(SLOTS, vision.shape[-1]), back.full[kind].reshape(SLOTS, HD))
-    total = to_x[lax.rem(y - x + NY, NY)].astype(F32)
-    landed = from_x.at[pl.ds(0, NX - 1)]
-    remote(landed, landed, sx.at[0], sx.at[1], head=x_peers[0]).wait_recv()
-    for slot in range(NX - 1):
-        total = total + from_x[slot].astype(F32)
-    grad_vision[...] = total.astype(BF)
-
-    remote(landed, landed, sx.at[0], sx.at[1], head=x_peers[0]).wait_send()
-    remote(far_weights, far_weights, sw.at[0], sw.at[1], head=far_head).wait_send()
+                far.arrived(0, off)
+            send_terms(off)
+
+    for off in range(NY):
+        back.last(0, off)
+    weight_grad(0, grad_w_key)
+
     scatter.finish()
     sums.finish()
     gather.finish(sums.from_z, sums.from_y)
@@ -602,20 +663,37 @@
     @pl.when(direct)
     def _():
         far.wait_sent(sums.from_y, far.sent.at[1])
-        far.wait_sent(far.full, far.sent.at[2])
+
+    @pl.when(relayed)
+    def _():
+        remote(near_weights, near_weights, sw.at[0], sw.at[1], head=far_head).wait_send()
 
     @pl.when(jnp.logical_and(relayed, is_owner(z)))
     def _():
         far.wait_sent(back.full.at[:, 0], far.sent.at[0])
 
-    save_attended.wait()
-    save_grad.wait()
+    def landed(count):
+        part = from_x.at[pl.ds(0, count)]
+        remote(part, part, sx.at[0], sx.at[1], head=x_peers[0]).wait_recv()
+        total = from_x[0].astype(F32)
+        for slot in range(1, count):
+            total = total + from_x[slot].astype(F32)
+        return total
+
+    @pl.when(direct)
+    def _():
+        sent = to_x.at[pl.ds(0, NC * NY - 1)]
+        remote(sent, sent, sx.at[0], sx.at[1], head=x_peers[0]).wait_send()
+        grad_vision[...] = (landed(NX - 1) + to_x[NC * lax.rem(y - x + NY, NY)].astype(F32)).astype(BF)
+
+    @pl.when(relayed)
+    def _():
+        grad_vision[...] = landed(NX).astype(BF)
 
 
 def cross(tile_turn, tile_len, query, grad_out, vision, w_key, w_value, text_turn, q_gain, k_gain):
     vmem = pl.BlockSpec(memory_space=pltpu.VMEM)
-    smem = pl.BlockSpec(memory_space=pltpu.SMEM)
-    hbm = pl.BlockSpec(memory_space=pl.ANY)
+    hbm = pl.BlockSpec(memory_space=pltpu.HBM)
     rows, columns = query.shape
     heads = columns // HD
     width = vision.shape[1]
@@ -628,14 +706,20 @@
             jax.ShapeDtypeStruct((width, HD), F32),
             jax.ShapeDtypeStruct((width, HD), F32),
         ),
-        in_specs=[smem, smem, hbm, hbm] + [vmem] * 6,
-        out_specs=(hbm, hbm) + (vmem,) * 3,
+        in_specs=[hbm] * 10,
+        out_specs=(vmem,) * 5,
         scratch_shapes=[
             pltpu.VMEM((rows, columns), BF),
             pltpu.VMEM((rows, columns), BF),
-            pltpu.VMEM((rows, columns), BF),
-            pltpu.VMEM((rows, columns), BF),
-            pltpu.SemaphoreType.DMA((4,)),
+            pltpu.VMEM((NC, NY, CHUNK, width), BF),
+            pltpu.VMEM((width, HD), BF),
+            pltpu.VMEM((width, HD), BF),
+            pltpu.VMEM((rows // HD, HD), jnp.int32),
+            pltpu.VMEM((1, HD), F32),
+            pltpu.VMEM((1, HD), F32),
+            pltpu.SMEM((SLOTS // TILE_TOK,), jnp.int32),
+            pltpu.SMEM((SLOTS // TILE_TOK,), jnp.int32),
+            pltpu.SemaphoreType.DMA((10,)),
             pltpu.VMEM((heads, rows, 2 * HD), BF),
             pltpu.VMEM((heads, rows, 2 * HD), BF),
             pltpu.VMEM((SLOTS, 2 * HD), BF),
@@ -644,15 +728,20 @@
             pltpu.VMEM((heads, rows, SLOTS), BF),
             pltpu.VMEM((2, HD, SLOTS), F32),
             pltpu.VMEM((HD, 2 * HD), BF),
+            pltpu.VMEM((width, SLOTS), BF),
+            pltpu.VMEM((NY, CHUNK, NC * width), F32),
             pltpu.VMEM((2, NY, CHUNK, HD), BF),
             pltpu.VMEM((2, NY, CHUNK, HD), F32),
             pltpu.VMEM((SHARD, HD), F32),
             pltpu.VMEM((2, NC, NY, CHUNK, HD), BF),
-            pltpu.VMEM((NY, CHUNK, width), BF),
+            pltpu.VMEM((NY * NC, CHUNK, width), BF),
             pltpu.VMEM((NX, CHUNK, width), BF),
-            pltpu.VMEM((2, width, HD), BF),
+            pltpu.VMEM((2, NC, width, HD), BF),
+            pltpu.VMEM((2, NC, width, HD), BF),
             pltpu.SemaphoreType.DMA((2,)),
             pltpu.SemaphoreType.DMA((2,)),
+            pltpu.SemaphoreType.DMA((2,)),
+            pltpu.SemaphoreType.REGULAR,
             pltpu.SemaphoreType.REGULAR,
             pltpu.SemaphoreType.REGULAR,
         ]
@@ -661,43 +750,39 @@
         compiler_params=pltpu.CompilerParams(collective_id=0, has_side_effects=True, vmem_limit_bytes=VMEM_LIMIT),
         name="cross",
     )(
-        tile_turn, tile_len, query, grad_out, vision.reshape(NC, NY, CHUNK, width), w_key, w_value, text_turn, q_gain, k_gain
+        *(
+            pltpu.with_memory_space_constraint(operand, pltpu.HBM)
+            for operand in (
+                tile_turn, tile_len, query, grad_out, vision.reshape(NC, NY, CHUNK, width), w_key, w_value, text_turn,
+                q_gain, k_gain,
+            )
+        )
     )
 
 
 def emit_kernel(*refs):
-    count = len(refs) // 3
-    sources, outs, held, sems = refs[:count], refs[count : 2 * count], refs[2 * count : 3 * count], refs[-1]
-    pieces = []
+    count = len(refs) // 2
+    copies = []
     for i in range(count):
-        rows = sources[i].shape[0]
-        for start in range(0, rows, CHUNK):
+        for start in range(0, refs[i].shape[0], CHUNK):
             part = pl.ds(start, CHUNK)
-            n = len(pieces)
-            pieces.append(
-                (
-                    pltpu.make_async_copy(sources[i].at[part], held[i].at[part], sems.at[0, n]),
-                    pltpu.make_async_copy(held[i].at[part], outs[i].at[part], sems.at[1, n]),
-                )
-            )
-    for into, _ in pieces:
-        into.start()
-    for into, out in pieces:
-        into.wait()
-        out.start()
-    for _, out in pieces:
-        out.wait()
+            copies.append(pltpu.make_async_copy(refs[i].at[part], refs[count + i].at[part], refs[-1].at[len(copies)]))
+    for copy in copies:
+        copy.start()
+    for copy in copies:
+        copy.wait()
 
 
 def emit(arrays):
-    hbm = pl.BlockSpec(memory_space=pl.ANY)
-    pieces = sum(a.shape[0] // CHUNK for a in arrays)
+    vmem = pl.BlockSpec(memory_space=pltpu.VMEM)
+    hbm = pl.BlockSpec(memory_space=pltpu.HBM)
     return pl.pallas_call(
         emit_kernel,
         out_shape=tuple(jax.ShapeDtypeStruct(a.shape, a.dtype) for a in arrays),
-        in_specs=[hbm] * len(arrays),
+        in_specs=[vmem] * len(arrays),
         out_specs=(hbm,) * len(arrays),
-        scratch_shapes=[pltpu.VMEM(a.shape, a.dtype) for a in arrays] + [pltpu.SemaphoreType.DMA((2, pieces))],
+        scratch_shapes=[pltpu.SemaphoreType.DMA((sum(a.shape[0] // CHUNK for a in arrays),))],
+        compiler_params=pltpu.CompilerParams(vmem_limit_bytes=8 * 1024 * 1024),
         name="emit",
     )(*arrays)
 

time: 82.2 us -> 77.1 us (0.938)
  the two profiles are of different devices: /device:TPU:9 before, /device:TPU:3 now
where the time goes in v4:
time: 77.1 us; the launch traced here: 76.6 us
  Pallas kernels  76 us (99%)
    pallas_call x1, Pallas kernels, cross(): pl.pallas_call(cross_kernel, out_shape=(jax.ShapeDtypeStruct(query.shape,...  74.5 us

profile of v4, /device:TPU:3, one launch (start us, length us, event | category | flops | bytes accessed | tf_op | source)
XLA Modules:
  0.0 76.6 jit_solution(2474972731509084610)
XLA Ops:
  0.6 74.5 %cross.1 = (bf16[512,1024]{1,0:T(8,128)(2,1)S(1)}, bf16[512,1024]{1,0:T(8,128)(2,1)S(1)}, bf16[128,128]{1,0:T(8,128)(2,1)S(1)}, f32[128,128]{1,0:T(8,128)S(1)}, f32[128,128]{1,0:T(8,128)S(1)}) custom-call(s32[4]{0:T(128)} %tile_turn_in.1, s32[4]{0:T(128)} %tile_len_in.1, bf16[512,1024]{1,0:T(8,128)(2,1)} %query.1, bf16[512,1024]{1,0:T(8,128)(2,1)} %grad_out.1, ...), custom_call_target="tpu_custom_call" | custom-call | tf_op jit(solution)/shard_map/cross/pallas_call | solution.py:700
  75.1 1.5 %emit.1 = (bf16[512,1024]{1,0:T(8,128)(2,1)}, bf16[512,1024]{1,0:T(8,128)(2,1)}, bf16[128,128]{1,0:T(8,128)(2,1)}, f32[128,128]{1,0:T(8,128)}, f32[128,128]{1,0:T(8,128)}) custom-call(bf16[512,1024]{1,0:T(8,128)(2,1)S(1)} %get-tuple-element.10.refs_0_, bf16[512,1024]{1,0:T(8,128)(2,1)S(1)} %get-tuple-element.11.refs_1_, ...), custom_call_target="tpu_custom_call" | custom-call | tf_op jit(solution)/shard_map/emit/pallas_call | solution.py:779

commit v5 on v4

--- a/solution.py
+++ b/solution.py
@@ -53,16 +53,21 @@
     )
 
 
+def nearest(z, step):
+    far = z // (NZ // 2)
+    return step * (1 - far) + (OWNERS - 1 - step) * far
+
+
 def scatter_scratch():
     return [
         pltpu.VMEM((2, NY, CHUNK, HD), BF),
-        pltpu.VMEM((2, NY, CHUNK, HD), BF),
-        pltpu.VMEM((2, NY - 1, CHUNK, HD), BF),
+        pltpu.VMEM((2, NY, OWNERS, SHARD, HD), BF),
+        pltpu.VMEM((2, OWNERS, NY - 1, SHARD, HD), BF),
         pltpu.VMEM((2, OWNERS, SHARD, HD), F32),
         pltpu.VMEM((2, OWNERS, SHARD, HD), BF),
         pltpu.VMEM((2, NZ - 1, SHARD, HD), BF),
         pltpu.SemaphoreType.DMA((2, NY)),
-        pltpu.SemaphoreType.DMA((2,)),
+        pltpu.SemaphoreType.DMA((2, OWNERS)),
         pltpu.SemaphoreType.DMA((2,)),
         pltpu.SemaphoreType.DMA((3,)),
     ]
@@ -71,7 +76,7 @@
 def gather_scratch():
     return [
         pltpu.VMEM((2, NC, NY, OWNERS, SHARD, HD), BF),
-        pltpu.SemaphoreType.DMA((2,)),
+        pltpu.SemaphoreType.DMA((2, OWNERS)),
         pltpu.SemaphoreType.DMA((2, NY)),
         pltpu.SemaphoreType.DMA((2, NY)),
         pltpu.SemaphoreType.DMA((3,)),
@@ -81,7 +86,7 @@
 def foreign_scratch():
     return [
         pltpu.VMEM((2, NY, OWNERS, SHARD, HD), BF),
-        pltpu.SemaphoreType.DMA((2,)),
+        pltpu.SemaphoreType.DMA((2, OWNERS)),
         pltpu.SemaphoreType.DMA((2, NY)),
         pltpu.SemaphoreType.DMA((2,)),
     ]
@@ -107,13 +112,17 @@
             yy = lax.rem(y + off, NY)
             self.core_copy(kind, off).wait_recv()
             both = self.own(kind, yy).astype(F32) + self.from_c[kind, yy].astype(F32)
+            both = both.reshape(OWNERS, SHARD, HD)
             if off == 0:
-                self.total[kind] = both.reshape(OWNERS, SHARD, HD)
+                self.total[kind] = both
             else:
                 self.to_y[kind, off] = both.astype(BF)
+        for step in reversed(range(OWNERS)):
+            owner = nearest(z, step)
+            for off in Y_ORDER:
                 remote(
-                    self.to_y.at[kind, off], self.from_y.at[kind, off - 1], self.sent.at[1], self.ry.at[kind],
-                    turn=turn_of(yy, z, core),
+                    self.to_y.at[kind, off, owner], self.from_y.at[kind, owner, off - 1], self.sent.at[1],
+                    self.ry.at[kind, owner], turn=turn_of(lax.rem(y + off, NY), z, core),
                 ).start()
 
     def wait(self, ref, sem):
@@ -126,16 +135,14 @@
 
     def over_y(self, kind):
         y, z, core = place()
-        self.wait(self.from_y.at[kind], self.ry.at[kind])
-        total = self.total[kind].reshape(CHUNK, HD)
-        for off in range(1, NY):
-            total = total + self.from_y[kind, off - 1].astype(F32)
-        total = total.reshape(OWNERS, SHARD, HD)
-        self.total[kind] = total
-        self.to_z[kind] = total.astype(BF)
-        far = z // (NZ // 2)
-        for step in range(OWNERS):
-            owner = (OWNERS - 1 - step) * (1 - far) + step * far
+        for step in reversed(range(OWNERS)):
+            owner = nearest(z, step)
+            self.wait(self.from_y.at[kind, owner], self.ry.at[kind, owner])
+            total = self.total[kind, owner]
+            for off in range(1, NY):
+                total = total + self.from_y[kind, owner, off - 1].astype(F32)
+            self.total[kind, owner] = total
+            self.to_z[kind, owner] = total.astype(BF)
 
             @pl.when(owner + OWN_LO != z)
             def _(owner=owner):
@@ -180,9 +187,15 @@
     def over_z(self, kind, shard):
         y, z, core = place()
         self.full[kind, core, y, z - OWN_LO] = shard.astype(BF)
+        self.send_z(kind)
+
+    def send_z(self, kind):
+        y, z, core = place()
         src = self.full.at[kind, core, y, z - OWN_LO]
         for off in (4, 3, 5, 2, 6, 1, 7):
-            remote(src, src, self.sent.at[0], self.rz.at[kind], turn=turn_of(y, lax.rem(z + off, NZ), core)).start()
+            remote(
+                src, src, self.sent.at[0], self.rz.at[kind, z - OWN_LO], turn=turn_of(y, lax.rem(z + off, NZ), core)
+            ).start()
 
     def wait(self, ref, sem):
         y, z, core = place()
@@ -194,28 +207,21 @@
 
     def over_y(self, kind):
         y, z, core = place()
-
-        @pl.when(is_owner(z))
-        def _():
-            self.wait(self.full.at[kind, core, y, OWN_LO + OWNERS - 1 - z], self.rz.at[kind])
-
-        @pl.when(jnp.logical_not(is_owner(z)))
-        def _():
-            self.wait(self.chunk(kind, core, y), self.rz.at[kind])
-
-        self.spread(kind)
-
-    def spread_y(self, kind):
-        y, z, core = place()
-        src = self.chunk(kind, core, y)
+        for step in range(OWNERS):
+            owner = nearest(z, step)
+
+            @pl.when(z != owner + OWN_LO)
+            def _(owner=owner):
+                self.wait(self.full.at[kind, core, y, owner], self.rz.at[kind, owner])
+
+            src = self.full.at[kind, core, y, owner]
+            self.spread_y(kind, src)
+            remote(src, src, self.sent.at[2], self.rc.at[kind, 0], turn=turn_of(y, z, 1 - core)).start()
+
+    def spread_y(self, kind, src):
+        y, z, core = place()
         for off in Y_ORDER:
             remote(src, src, self.sent.at[1], self.ry.at[kind, off], turn=turn_of(lax.rem(y + off, NY), z, core)).start()
-
-    def spread(self, kind):
-        y, z, core = place()
-        self.spread_y(kind)
-        src = self.chunk(kind, core, y)
-        remote(src, src, self.sent.at[2], self.rc.at[kind, 0], turn=turn_of(y, z, 1 - core)).start()
 
     def over_core(self, kind, off):
         y, z, core = place()
@@ -247,16 +253,19 @@
 
     def over_z(self, kind, src, head):
         y, z, core = place()
-        for zz in range(NZ):
+        for off in (0, 1, 7, 2, 6, 3, 5, 4):
             remote(
-                src, self.full.at[kind, y, z - OWN_LO], self.sent.at[0], self.rz.at[kind],
-                turn=turn_of(y, zz, core), head=head,
+                src, self.full.at[kind, y, z - OWN_LO], self.sent.at[0], self.rz.at[kind, z - OWN_LO],
+                turn=turn_of(y, lax.rem(z + off, NZ), core), head=head,
             ).start()
 
     def over_y(self, kind):
         y, z, core = place()
-        self.wait(self.full.at[kind, y], self.rz.at[kind])
-        self.spread_y(kind)
+        for step in reversed(range(OWNERS)):
+            owner = nearest(z, step)
+            src = self.full.at[kind, y, owner]
+            self.wait(src, self.rz.at[kind, owner])
+            self.spread_y(kind, src)
 
     def arrived(self, kind, off):
         y, z, core = place()
@@ -395,6 +404,7 @@
         near_weights[kind, 0] = weight[...]
         remote(weight, near_weights.at[kind, 1], sn.at[0], sn.at[1], turn=turn_of(y, z, 1 - core)).start()
     scatter.over_core(0)
+    scatter.over_core(1)
     for load in loads[3:]:
         load.wait()
     for tile in range(SLOTS // TILE_TOK):
@@ -413,15 +423,14 @@
 
     lax.fori_loop(0, 3, norm_queries, 0)
     scatter.over_y(0)
-    scatter.over_core(1)
     lax.fori_loop(3, heads, norm_queries, 0)
+    scatter.over_y(1)
 
     def key_shard(total):
         raw[...] = total
         gather.over_z(0, total * inverse_rms(total) * k_gain[...])
 
     scatter.over_z(0, key_shard)
-    scatter.over_y(1)
     gather.over_y(0)
     scatter.over_z(1, lambda total: gather.over_z(1, total))
     for off in Y_ARRIVAL:
@@ -542,11 +551,13 @@
     put(0, 1.0 / LOG2E)
 
     def spread(kind, total):
-        back.over_z(kind, total)
+        back.full[kind, core, y, z - OWN_LO] = total.astype(BF)
 
         @pl.when(core != hi)
         def _():
             far.over_z(kind, back.full.at[kind, core, y, z - OWN_LO], far_head)
+
+        back.send_z(kind)
 
     def query_grad(h):
         d_query = jnp.dot(expo[h], ka[:, :HD], preferred_element_type=F32)

time: 77.1 us -> 75.9 us (0.984)
  the two profiles are of different devices: /device:TPU:3 before, /device:TPU:4 now
where the time goes in v5:
time: 75.9 us; the launch traced here: 75.8 us
  Pallas kernels  75.2 us (99%)
    pallas_call x1, Pallas kernels, cross(): pl.pallas_call(cross_kernel, out_shape=(jax.ShapeDtypeStruct(query.shape,...  73.7 us

profile of v5, /device:TPU:4, one launch (start us, length us, event | category | flops | bytes accessed | tf_op | source)
XLA Modules:
  0.0 75.8 jit_solution(9195726769123261139)
XLA Ops:
  0.6 73.7 %cross.1 = (bf16[512,1024]{1,0:T(8,128)(2,1)S(1)}, bf16[512,1024]{1,0:T(8,128)(2,1)S(1)}, bf16[128,128]{1,0:T(8,128)(2,1)S(1)}, f32[128,128]{1,0:T(8,128)S(1)}, f32[128,128]{1,0:T(8,128)S(1)}) custom-call(s32[4]{0:T(128)} %tile_turn_in.1, s32[4]{0:T(128)} %tile_len_in.1, bf16[512,1024]{1,0:T(8,128)(2,1)} %query.1, bf16[512,1024]{1,0:T(8,128)(2,1)} %grad_out.1, ...), custom_call_target="tpu_custom_call" | custom-call | tf_op jit(solution)/shard_map/cross/pallas_call | solution.py:711
  74.4 1.5 %emit.1 = (bf16[512,1024]{1,0:T(8,128)(2,1)}, bf16[512,1024]{1,0:T(8,128)(2,1)}, bf16[128,128]{1,0:T(8,128)(2,1)}, f32[128,128]{1,0:T(8,128)}, f32[128,128]{1,0:T(8,128)}) custom-call(bf16[512,1024]{1,0:T(8,128)(2,1)S(1)} %get-tuple-element.10.refs_0_, bf16[512,1024]{1,0:T(8,128)(2,1)S(1)} %get-tuple-element.11.refs_1_, ...), custom_call_target="tpu_custom_call" | custom-call | tf_op jit(solution)/shard_map/emit/pallas_call | solution.py:790

commit v6 on v5

--- a/solution.py
+++ b/solution.py
@@ -447,7 +447,7 @@
         score(2 * pair)
         score(2 * pair + 1)
 
-        @pl.when(pair == 1)
+        @pl.when(pair == 2)
         def _():
             for off in Y_ARRIVAL:
                 gather.over_core(1, off)
@@ -576,10 +576,6 @@
         def _():
             sums.over_core(0)
 
-        @pl.when(pair == 2)
-        def _():
-            sums.over_z(1, lambda total: spread(1, total))
-
         @pl.when(pair == 3)
         def _():
             sums.over_y(0)
@@ -599,6 +595,7 @@
             - raw_values * (inverse * inverse * inverse) * jnp.mean(raw_values * scaled, axis=1, keepdims=True),
         )
 
+    sums.over_z(1, lambda total: spread(1, total))
     sums.over_z(0, key_grad_shard)
     def far_over_y(kind):
         @pl.when(direct)

time: 75.9 us -> 75 us (0.988)
  the two profiles are of different devices: /device:TPU:4 before, /device:TPU:34 now
where the time goes in v6:
time: 75 us; the launch traced here: 74.9 us
  Pallas kernels  74.3 us (99%)
    pallas_call x1, Pallas kernels, cross(): pl.pallas_call(cross_kernel, out_shape=(jax.ShapeDtypeStruct(query.shape,...  72.8 us

profile of v6, /device:TPU:34, one launch (start us, length us, event | category | flops | bytes accessed | tf_op | source)
XLA Modules:
  0.0 74.9 jit_solution(17886725911544051998)
XLA Ops:
  0.6 72.8 %cross.1 = (bf16[512,1024]{1,0:T(8,128)(2,1)S(1)}, bf16[512,1024]{1,0:T(8,128)(2,1)S(1)}, bf16[128,128]{1,0:T(8,128)(2,1)S(1)}, f32[128,128]{1,0:T(8,128)S(1)}, f32[128,128]{1,0:T(8,128)S(1)}) custom-call(s32[4]{0:T(128)} %tile_turn_in.1, s32[4]{0:T(128)} %tile_len_in.1, bf16[512,1024]{1,0:T(8,128)(2,1)} %query.1, bf16[512,1024]{1,0:T(8,128)(2,1)} %grad_out.1, ...), custom_call_target="tpu_custom_call" | custom-call | tf_op jit(solution)/shard_map/cross/pallas_call | solution.py:708
  73.5 1.5 %emit.1 = (bf16[512,1024]{1,0:T(8,128)(2,1)}, bf16[512,1024]{1,0:T(8,128)(2,1)}, bf16[128,128]{1,0:T(8,128)(2,1)}, f32[128,128]{1,0:T(8,128)}, f32[128,128]{1,0:T(8,128)}) custom-call(bf16[512,1024]{1,0:T(8,128)(2,1)S(1)} %get-tuple-element.10.refs_0_, bf16[512,1024]{1,0:T(8,128)(2,1)S(1)} %get-tuple-element.11.refs_1_, ...), custom_call_target="tpu_custom_call" | custom-call | tf_op jit(solution)/shard_map/emit/pallas_call | solution.py:787
